TPU v7x, 32 devices: a whole 2x2x4 slice. The times are simulated.
32 devices in a mesh: mode: 4 (over z), ty: 4 (over y, core), tx: 2 (over x).
Axes of the slice: x: 2, y: 2, z: 4, core: 2. Of those that a mesh axis runs over, the one named last changes fastest.
Arguments:
- object_slices: float32 [4, 2, 512, 256], P(None, None, 'ty', 'tx'), may hold values from -4.2 to 4.2
- probe_modes: float32 [16, 2, 128, 128], P('mode'), may hold values from -1.5 to 1.5
- positions: int32 [4, 2, 1, 2], P('ty', 'tx'), may hold values from 0 to 128
- measured: float32 [4, 2, 1, 128, 128], P('ty', 'tx'), may hold values from 0.3 to 3
Outputs:
- object_gradient: float32 [4, 2, 512, 256], P('mode', None, 'ty', 'tx')
Inputs may be any that keep to these rules, and one draw needn't show every extreme that they name: `positions`: pattern k of tile (a, b) has its 128 x 128 window inside that tile's region, which reaches 64 pixels beyond the tile on every side.
All inputs are finite; a program needn't handle non-finite values.
Results may differ from a plain program's by a relative error of at most 0.00016.
Values sent between devices are 32-bit elements; how exact they have to be, the bound alone decides.
No kernel may reach another device: no remote copies, remote signals or barrier semaphores. Data moves between devices by JAX's collectives and lax.ppermute only.
A program may use at most 64 MiB of HBM per device.

v0:
```python
import functools

import jax
import jax.numpy as jnp
import numpy as np
from jax import lax
from jax.experimental import pallas as pl
from jax.experimental.pallas import tpu as pltpu
from jax.sharding import PartitionSpec as P

FRESNEL_RATE = 0.3
F32, BF16 = jnp.float32, jnp.bfloat16
VMEM_LIMIT = 40 * 2**20


def pair(high, low):
    first = high.astype(jnp.bfloat16)
    return [first, (low - first.astype(np.float64)).astype(jnp.bfloat16)]


def tables(length):
    counter = np.arange(length)
    fourier = np.exp(-2j * np.pi / length * (np.outer(counter, counter) % length)) / np.sqrt(length)
    frequency = np.where(counter < length // 2, counter, counter - length).astype(np.float64)
    chirp = np.exp(-1j * FRESNEL_RATE * frequency**2 / length)
    moved = fourier.conj() @ (chirp[:, None] * fourier)
    stacked = []
    for matrix in (moved, fourier):
        right = np.block([[matrix.real, matrix.imag], [-matrix.imag, matrix.real]])
        stacked += pair(right, right) + pair(right.T, right.T)
    return np.stack(stacked)


def dot(left, right):
    return jnp.dot(left, right, preferred_element_type=F32)


def split(value):
    high = value.astype(BF16)
    return high, (value - high.astype(F32)).astype(BF16)


def two_sided(planes, table_ref, base, conjugate):
    det = planes[0][0].shape[0]
    right, left = (base + 2, base) if conjugate else (base, base + 2)
    field = jnp.concatenate([jnp.concatenate(mode, 1) for mode in planes], 0)
    high, low = split(field)
    upper = dot(high, table_ref[right]) + dot(low, table_ref[right]) + dot(high, table_ref[right + 1])
    columns = []
    for part in split(upper):
        first, second = part[:det], part[det:]
        real = jnp.concatenate([first[:, :det], second[:, :det]], 1)
        imag = jnp.concatenate([first[:, det:], second[:, det:]], 1)
        columns.append(jnp.concatenate([real, imag], 0))
    high, low = columns
    both = dot(table_ref[left], high) + dot(table_ref[left], low) + dot(table_ref[left + 1], high)
    return [(both[:det, j * det : (j + 1) * det], both[det:, j * det : (j + 1) * det]) for j in range(2)]


def iota(shape, dim):
    return lax.broadcasted_iota(jnp.int32, shape, dim)


def half_roll(plane):
    return pltpu.roll(plane, plane.shape[1] // 2, 1)


def is_right(index, parity):
    return lax.rem(index, 2) == parity


def window_rows(above, tile, below, start):
    det = tile.shape[0]
    half = det // 2
    first = jnp.concatenate([above, tile[:half]], 0)
    second = jnp.concatenate([tile[half:], below], 0)
    mixed = jnp.where(iota(first.shape, 0) >= start, first, second)
    return pltpu.roll(mixed, lax.rem(det - start, det), 0)


def pack_kernel(parities, column_axis, tile_ref, above_ref, below_ref, *refs):
    count = len(parities)
    place_refs, message_refs = refs[:count], refs[count:]
    column = lax.axis_index(column_axis)
    for parity, place_ref, message_ref in zip(parities, place_refs, message_refs):
        start = place_ref[0]
        right = is_right(column, parity)
        for s in range(tile_ref.shape[0]):
            real, imag = [window_rows(above_ref[s, c], tile_ref[s, c], below_ref[s, c], start) for c in range(2)]
            lower = iota(real.shape, 1) < real.shape[1] // 2
            to_right = jnp.where(lower, half_roll(real), imag)
            to_left = jnp.where(lower, real, half_roll(imag))
            message_ref[s] = jnp.where(right, to_right, to_left)


def forward_kernel(parities, column_axis, place_ref, tile_ref, above_ref, below_ref, table_ref, *refs):
    count = len(parities)
    message_refs, probe_refs = refs[:count], refs[count : count + 3]
    window_ref, wave_ref, far_ref, intensity_ref = refs[count + 3 :]
    slices, _, det, _ = tile_ref.shape
    row, col = place_ref[0], place_ref[1]
    column = lax.axis_index(column_axis)
    lanes = iota((det, det), 1)
    lower = lanes < det // 2
    late = lanes >= col
    back_shift = lax.rem(det - col, det)
    probes = [(ref, j) for ref in probe_refs for j in range(ref.shape[0])]
    for s in range(slices):
        messages = [ref[s] for ref in message_refs]
        for c in range(2):
            own = half_roll(window_rows(above_ref[s, c], tile_ref[s, c], below_ref[s, c], row))
            left, right = jnp.zeros_like(own), jnp.zeros_like(own)
            for parity, message in zip(parities, messages):
                turned = half_roll(message)
                at_right = is_right(column, parity)
                right = right + jnp.where(at_right, turned if c == 0 else message, 0.0)
                left = left + jnp.where(at_right, 0.0, message if c == 0 else turned)
            early_block = jnp.where(lower, left, own)
            late_block = jnp.where(lower, own, right)
            window_ref[s, c] = pltpu.roll(jnp.where(late, early_block, late_block), back_shift, 1)
    total = jnp.zeros((det, det), F32)
    for s in range(slices):
        real, imag = window_ref[s, 0], window_ref[s, 1]
        for first in range(0, len(probes), 2):
            planes = []
            for mode in (first, first + 1):
                if s == 0:
                    ref, j = probes[mode]
                    wave_real, wave_imag = ref[j, 0], ref[j, 1]
                else:
                    wave_real, wave_imag = wave_ref[s - 1, mode, 0], wave_ref[s - 1, mode, 1]
                planes.append((wave_real * real - wave_imag * imag, wave_real * imag + wave_imag * real))
            last = s == slices - 1
            result = two_sided(planes, table_ref, 4 if last else 0, False)
            for j, (out_real, out_imag) in enumerate(result):
                target = far_ref.at[first + j] if last else wave_ref.at[s, first + j]
                target[0] = out_real
                target[1] = out_imag
                if last:
                    total = total + (out_real * out_real + out_imag * out_imag)
    intensity_ref[...] = total


def backward_kernel(parities, mode_axis, column_axis, place_ref, measured_ref, mine_ref, other_ref, table_ref, *refs):
    count = len(parities)
    probe_refs, (window_ref, wave_ref, far_ref) = refs[:3], refs[3:6]
    center_ref, send_ref = refs[6:8]
    strip_refs, send_strip_refs = refs[8 : 8 + count], refs[8 + count : 8 + 2 * count]
    keep_ref, back_ref = refs[8 + 2 * count :]
    slices, _, det, _ = window_ref.shape
    modes = far_ref.shape[0]
    col = place_ref[1]
    me = lax.axis_index(mode_axis)
    peer = me + 1 - 2 * lax.rem(me, 2)
    column = lax.axis_index(column_axis)
    probes = [(ref, j) for ref in probe_refs for j in range(ref.shape[0])]
    intensity = mine_ref[...] + other_ref[...]
    weight = 1.0 - measured_ref[...] / jnp.maximum(jnp.sqrt(intensity), 1.0)
    for s in reversed(range(slices)):
        last = s == slices - 1
        term_real, term_imag = jnp.zeros((det, det), F32), jnp.zeros((det, det), F32)
        if not last:
            real, imag = window_ref[s + 1, 0], window_ref[s + 1, 1]
        for first in range(0, modes, 2):
            planes = []
            for mode in (first, first + 1):
                if last:
                    planes.append((weight * far_ref[mode, 0], weight * far_ref[mode, 1]))
                else:
                    back_real, back_imag = back_ref[mode, 0], back_ref[mode, 1]
                    planes.append((real * back_real + imag * back_imag, real * back_imag - imag * back_real))
            result = two_sided(planes, table_ref, 4 if last else 0, True)
            for j, (back_real, back_imag) in enumerate(result):
                mode = first + j
                if s > 0:
                    back_ref[mode, 0] = back_real
                    back_ref[mode, 1] = back_imag
                    wave_real, wave_imag = wave_ref[s - 1, mode, 0], wave_ref[s - 1, mode, 1]
                else:
                    ref, k = probes[mode]
                    wave_real, wave_imag = ref[k, 0], ref[k, 1]
                term_real = term_real + (wave_real * back_real + wave_imag * back_imag)
                term_imag = term_imag + (wave_real * back_imag - wave_imag * back_real)
        for slot, owner in ((0, me), (1, peer)):

            @pl.when(owner == s)
            def _(slot=slot, term_real=term_real, term_imag=term_imag):
                keep_ref[slot, 0] = term_real
                keep_ref[slot, 1] = term_imag

    lanes = iota((det, det), 1)
    lower, late = lanes < det // 2, lanes >= col
    forth_shift = lax.rem(col, det)
    for slot, middle_ref, out_strip_refs in ((0, center_ref, strip_refs), (1, send_ref, send_strip_refs)):
        early, latter = [], []
        for c in range(2):
            turned = pltpu.roll(keep_ref[slot, c], forth_shift, 1)
            early.append(jnp.where(late, turned, 0.0))
            latter.append(jnp.where(late, 0.0, turned))
            middle_ref[c] = half_roll(jnp.where(lower, latter[c], early[c]))
        to_right = jnp.where(lower, half_roll(latter[0]), latter[1])
        to_left = jnp.where(lower, early[0], half_roll(early[1]))
        for parity, strip_ref in zip(parities, out_strip_refs):
            strip_ref[...] = jnp.where(is_right(column, parity), to_right, to_left)


def place_kernel(parities, column_axis, place_ref, mine_ref, other_ref, *refs):
    count = len(parities)
    place_refs, one_refs, two_refs = refs[:count], refs[count : 2 * count], refs[2 * count : 3 * count]
    middle_ref, up_ref, down_ref = refs[3 * count :]
    det = mine_ref.shape[1]
    half = det // 2
    column = lax.axis_index(column_axis)
    rows, lower = iota((det, det), 0), iota((det, det), 1) < half
    start = place_ref[0]

    def placed(plane, begin):
        turned = pltpu.roll(plane, lax.rem(begin, det), 0)
        late = rows >= begin
        return jnp.where(late, turned, 0.0), jnp.where(late, 0.0, turned)

    blocks = [list(placed(mine_ref[c] + other_ref[c], start)) for c in range(2)]
    for parity, partner_ref, one_ref, two_ref in zip(parities, place_refs, one_refs, two_refs):
        strip = one_ref[...] + two_ref[...]
        at_right = is_right(column, parity)
        for block, part in enumerate(placed(strip, partner_ref[0])):
            turned = half_roll(part)
            real = jnp.where(lower != at_right, jnp.where(at_right, turned, part), 0.0)
            imag = jnp.where(lower != at_right, jnp.where(at_right, part, turned), 0.0)
            blocks[0][block] = blocks[0][block] + real
            blocks[1][block] = blocks[1][block] + imag
    for c in range(2):
        first, second = blocks[c]
        up_ref[c] = first[:half]
        middle_ref[c, :half] = first[half:]
        middle_ref[c, half:] = second[:half]
        down_ref[c] = second[half:]


SMEM_SPEC = pl.BlockSpec(memory_space=pltpu.SMEM)
VMEM_SPEC = pl.BlockSpec(memory_space=pltpu.VMEM)


def call(kernel, outs, operands, scratch=(), scalars=()):
    return pl.pallas_call(
        kernel,
        out_shape=outs,
        in_specs=[SMEM_SPEC if i in scalars else VMEM_SPEC for i in range(len(operands))],
        out_specs=jax.tree.map(lambda _: VMEM_SPEC, outs),
        scratch_shapes=scratch,
        compiler_params=pltpu.CompilerParams(vmem_limit_bytes=VMEM_LIMIT),
    )(*operands)


def body(object_slices, probe_modes, positions, measured):
    modes_here, _, det, _ = probe_modes.shape
    slices, half = object_slices.shape[0], det // 2
    groups, height, width = lax.axis_size("mode"), lax.axis_size("ty"), lax.axis_size("tx")
    place = positions.reshape(2)

    upward = [(i, i - 1) for i in range(1, height)]
    downward = [(i - 1, i) for i in range(1, height)]
    parities = (0,) if width == 2 else (0, 1)

    def edges(parity):
        ends = [(i, i + 1) for i in range(parity, width - 1, 2)]
        return ends + [(j, i) for i, j in ends]

    mirror = [(i, groups - 1 - i) for i in range(groups)]
    neighbour = [(i, i ^ 1) for i in range(groups)]

    above = lax.ppermute(object_slices[:, :, half:], "ty", downward)
    below = lax.ppermute(object_slices[:, :, :half], "ty", upward)
    partner_places = [lax.ppermute(place, "tx", edges(parity)) for parity in parities]
    row_parity = lax.rem(lax.axis_index("ty"), 2)
    part = lax.dynamic_slice_in_dim(probe_modes, row_parity * (modes_here // 2), modes_here // 2, 0)
    far_half = lax.ppermute(part, "mode", mirror)
    swap = [(i, i ^ 1) for i in range(height)]
    near_half = lax.ppermute(far_half, "ty", swap)
    probes = [probe_modes, far_half, near_half]

    count = len(parities)
    message = jax.ShapeDtypeStruct((slices, det, det), F32)
    messages = call(
        functools.partial(pack_kernel, parities, "tx"),
        [message] * count,
        [object_slices, above, below, *partner_places],
        scalars=range(3, 3 + count),
    )
    messages = [lax.ppermute(block, "tx", edges(parity)) for parity, block in zip(parities, messages)]

    table = jnp.asarray(tables(det))
    modes = 2 * modes_here
    plane = jax.ShapeDtypeStruct((det, det), F32)
    complex_plane = jax.ShapeDtypeStruct((2, det, det), F32)
    window, wave, far, mine = call(
        functools.partial(forward_kernel, parities, "tx"),
        [
            jax.ShapeDtypeStruct((slices, 2, det, det), F32),
            jax.ShapeDtypeStruct((slices - 1, modes, 2, det, det), F32),
            jax.ShapeDtypeStruct((modes, 2, det, det), F32),
            plane,
        ],
        [place, object_slices, above, below, table, *messages, *probes],
        scalars=(0,),
    )
    other = lax.ppermute(mine, "mode", neighbour)
    center, send, *strips = call(
        functools.partial(backward_kernel, parities, "mode", "tx"),
        [complex_plane] * 2 + [plane] * (2 * count),
        [place, measured.reshape(det, det), mine, other, table, *probes, window, wave, far],
        scratch=[pltpu.VMEM((2, 2, det, det), F32), pltpu.VMEM((modes, 2, det, det), F32)],
        scalars=(0,),
    )
    received = lax.ppermute(send, "mode", neighbour)
    ones = [lax.ppermute(block, "tx", edges(parity)) for parity, block in zip(parities, strips[:count])]
    twos = []
    for parity, block in zip(parities, strips[count:]):
        route = [(i * width + p, j * width + q) for i, j in neighbour for p, q in edges(parity)]
        twos.append(lax.ppermute(block, ("mode", "tx"), route))
    strip = jax.ShapeDtypeStruct((2, half, det), F32)
    middle, up, down = call(
        functools.partial(place_kernel, parities, "tx"),
        [complex_plane, strip, strip],
        [place, center, received, *partner_places, *ones, *twos],
        scalars=(0, *range(3, 3 + count)),
    )
    from_below = lax.ppermute(up, "ty", upward)
    from_above = lax.ppermute(down, "ty", downward)
    return (middle + jnp.concatenate([from_above, from_below], 1))[None]


def solution(mesh):
    return jax.shard_map(
        body,
        mesh=mesh,
        in_specs=(
            P(None, None, "ty", "tx"),
            P("mode", None, None, None),
            P("ty", "tx", None, None),
            P("ty", "tx", None, None, None),
        ),
        out_specs=P("mode", None, "ty", "tx"),
        check_vma=False,
    )
```

profile of v0, /device:TPU:1, one launch (start us, length us, event | category | flops | bytes accessed | tf_op | source)
XLA Modules:
  0.0 61.4 jit_solution(7231259496075873374)
XLA Ops:
  0.0 0.0 copy-start.1
  0.0 0.0 copy-start.2
  0.0 1.1 %constant_dynamic-slice_fusion = f32[2,2,128,128]{3,2,1,0:T(8,128)S(1)} fusion(f32[4,2,128,128]{3,2,1,0:T(8,128)} %refs_0_.1, s32[]{:T(128)S(6)} %select_n.3), kind=kLoop, calls=%fused_computation.2 | loop fusion | bytes 524292 | tf_op jit(solution)/shard_map/dynamic_slice | solution.py:276
  1.1 4.2 %collective-permute-start.4 = (f32[2,2,128,128]{3,2,1,0:T(8,128)S(1)}, f32[2,2,128,128]{3,2,1,0:T(8,128)S(1)}, u32[]{:S(2)}, u32[]{:S(2)}) collective-permute-start(f32[2,2,128,128]{3,2,1,0:T(8,128)S(1)} %constant_dynamic-slice_fusion), channel_id=1, source_target_pairs={{0,24},{8,16},{16,8},{24,0},{1,25},{9,17},{17,9},{25,1},{2,26},{10... | collective-permute-start | bytes 786440 | tf_op jit(solution)/shard_map/ppermute | solution.py:277
  5.3 1.1 %fusion.1 = (f32[4,2,64,128]{3,2,1,0:T(8,128)S(1)}, f32[4,2,64,128]{3,2,1,0:T(8,128)S(1)}) fusion(f32[4,2,128,128]{3,2,1,0:T(8,128)} %tile_ref.3), kind=kLoop, calls=%fused_computation.3 | loop fusion | bytes 1048576 | tf_op jit(solution)/shard_map/slice | solution.py:273
  6.4 2.9 %collective-permute-start.1 = (f32[4,2,64,128]{3,2,1,0:T(8,128)S(1)}, f32[4,2,64,128]{3,2,1,0:T(8,128)S(1)}, u32[]{:S(2)}, u32[]{:S(2)}) collective-permute-start(f32[4,2,64,128]{3,2,1,0:T(8,128)S(1)} %get-tuple-element.27), channel_id=1, source_target_pairs={{2,0},{4,2},{6,4},{3,1},{5,3},{7,5},{10,8},{12,10},{14,12},{11,9},... | collective-permute-start | bytes 786440 | tf_op jit(solution)/shard_map/ppermute | solution.py:273
  9.3 3.0 %collective-permute-start = (f32[4,2,64,128]{3,2,1,0:T(8,128)S(1)}, f32[4,2,64,128]{3,2,1,0:T(8,128)S(1)}, u32[]{:S(2)}, u32[]{:S(2)}) collective-permute-start(f32[4,2,64,128]{3,2,1,0:T(8,128)S(1)} %get-tuple-element.28), channel_id=1, source_target_pairs={{0,2},{2,4},{4,6},{1,3},{3,5},{5,7},{8,10},{10,12},{12,14},{9,11},... | collective-permute-start | bytes 786440 | tf_op jit(solution)/shard_map/ppermute | solution.py:272
  12.3 1.3 %collective-permute-start.2 = (s32[2]{0:T(128)}, s32[2]{0:T(128)S(1)}, u32[]{:S(2)}, u32[]{:S(2)}) collective-permute-start(s32[2]{0:T(128)} %bitcast.5), channel_id=1, source_target_pairs={{0,1},{1,0},{2,3},{3,2},{4,5},{5,4},{6,7},{7,6},{8,9},{9,8},{10,11... | collective-permute-start | bytes 32 | tf_op jit(solution)/shard_map/ppermute | solution.py:274
  13.6 0.0 collective-permute-done.4.refs_2_.refs_1_
  13.6 0.0 collective-permute-start.5
  13.6 1.3 %collective-permute-done.2.refs_0_ = s32[2]{0:T(128)S(1)} collective-permute-done((s32[2]{0:T(128)}, s32[2]{0:T(128)S(1)}, u32[]{:S(2)}, u32[]{:S(2)}) %collective-permute-start.2) | collective-permute-done | bytes 40 | tf_op jit(solution)/shard_map/ppermute | solution.py:274
  14.9 0.0 collective-permute-done.1.below_ref
  14.9 0.7 %collective-permute-done.above_ref = f32[4,2,64,128]{3,2,1,0:T(8,128)S(1)} collective-permute-done((f32[4,2,64,128]{3,2,1,0:T(8,128)S(1)}, f32[4,2,64,128]{3,2,1,0:T(8,128)S(1)}, u32[]{:S(2)}, u32[]{:S(2)}) %collective-permute-start) | collective-permute-done | bytes 262176 | tf_op jit(solution)/shard_map/ppermute | solution.py:272
  15.6 0.0 copy-start
  15.6 1.0 %copy-done = f32[4,2,128,128]{3,2,1,0:T(8,128)S(1)} copy-done((f32[4,2,128,128]{3,2,1,0:T(8,128)S(1)}, f32[4,2,128,128]{3,2,1,0:T(8,128)}, u32[]{:S(2)}) %copy-start) | copy-done | bytes 524312
  16.6 0.0 copy-start.3
  16.7 0.9 %shard_map.55 = f32[4,128,128]{2,1,0:T(8,128)S(1)} custom-call(f32[4,2,128,128]{3,2,1,0:T(8,128)S(1)} %copy-done, f32[4,2,64,128]{3,2,1,0:T(8,128)S(1)} %collective-permute-done.above_ref, f32[4,2,64,128]{3,2,1,0:T(8,128)S(1)} %collective-permute-done.1.below_ref, s32[2]{0:T(128)S(1)} %collective-permute-done.2.refs_0_), custom_call_target="tpu_custom_call" | custom-call | tf_op jit(solution)/shard_map/pallas_call | solution.py:245
  17.6 1.3 %collective-permute-start.3 = (f32[4,128,128]{2,1,0:T(8,128)S(1)}, f32[4,128,128]{2,1,0:T(8,128)S(1)}, u32[]{:S(2)}, u32[]{:S(2)}) collective-permute-start(f32[4,128,128]{2,1,0:T(8,128)S(1)} %shard_map.55), channel_id=1, source_target_pairs={{0,1},{1,0},{2,3},{3,2},{4,5},{5,4},{6,7},{7,6},{8,9},{9,8},{10,11... | collective-permute-start | bytes 786440 | tf_op jit(solution)/shard_map/ppermute | solution.py:290
  18.8 0.0 collective-permute-done.5.refs_3_.refs_2_
  18.8 6.8 %collective-permute-done.3.refs_0_ = f32[4,128,128]{2,1,0:T(8,128)S(1)} collective-permute-done((f32[4,128,128]{2,1,0:T(8,128)S(1)}, f32[4,128,128]{2,1,0:T(8,128)S(1)}, u32[]{:S(2)}, u32[]{:S(2)}) %collective-permute-start.3) | collective-permute-done | bytes 262176 | tf_op jit(solution)/shard_map/ppermute | solution.py:290
  25.7 0.0 copy-done.1
  25.7 0.0 copy-done.2
  25.7 0.0 copy-start.4
  25.7 0.7 %copy-done.4 = s32[1,1,1,2]{3,2,1,0:T(1,128)S(1)} copy-done((s32[1,1,1,2]{3,2,1,0:T(1,128)S(1)}, s32[1,1,1,2]{3,2,1,0:T(1,128)}, u32[]{:S(2)}) %copy-start.4) | copy-done | bytes 32
  26.3 4.7 %shard_map.56 = (f32[4,2,128,128]{3,2,1,0:T(8,128)S(1)}, f32[3,8,2,128,128]{4,3,2,1,0:T(8,128)S(1)}, f32[8,2,128,128]{3,2,1,0:T(8,128)S(1)}, f32[128,128]{1,0:T(8,128)S(1)}) custom-call(s32[2]{0:T(128)S(1)} %bitcast.6, f32[4,2,128,128]{3,2,1,0:T(8,128)S(1)} %copy-done, f32[4,2,64,128]{3,2,1,0:T(8,128)S(1)} %collective-permute-done.above_ref, ...), custom_call_target="tpu_custom_call" | custom-call | tf_op jit(solution)/shard_map/pallas_call | solution.py:245
  31.0 2.0 %collective-permute-start.6 = (f32[128,128]{1,0:T(8,128)S(1)}, f32[128,128]{1,0:T(8,128)S(1)}, u32[]{:S(2)}, u32[]{:S(2)}) collective-permute-start(f32[128,128]{1,0:T(8,128)S(1)} %get-tuple-element.16.mine_ref), channel_id=1, source_target_pairs={{0,8},{8,0},{16,24},{24,16},{1,9},{9,1},{17,25},{25,17},{2,10},{10... | collective-permute-start | bytes 196616 | tf_op jit(solution)/shard_map/ppermute | solution.py:307
  33.0 1.7 %collective-permute-done.6.other_ref = f32[128,128]{1,0:T(8,128)S(1)} collective-permute-done((f32[128,128]{1,0:T(8,128)S(1)}, f32[128,128]{1,0:T(8,128)S(1)}, u32[]{:S(2)}, u32[]{:S(2)}) %collective-permute-start.6) | collective-permute-done | bytes 65568 | tf_op jit(solution)/shard_map/ppermute | solution.py:307
  34.7 0.0 copy-done.3
  34.7 6.4 %shard_map.57 = (f32[2,128,128]{2,1,0:T(8,128)S(1)}, f32[2,128,128]{2,1,0:T(8,128)S(1)}, f32[128,128]{1,0:T(8,128)S(1)}, f32[128,128]{1,0:T(8,128)S(1)}) custom-call(s32[2]{0:T(128)S(1)} %bitcast.7, f32[128,128]{1,0:T(8,128)S(1)} %bitcast.4, f32[128,128]{1,0:T(8,128)S(1)} %get-tuple-element.16.mine_ref, f32[128,128]{1,0:T(8,128)S(1)} %collective-permute-done.6.other_ref, ...), custom_call_target="tpu_custom_call" | custom-call | tf_op jit(solution)/shard_map/pallas_call | solution.py:245
  41.0 1.5 %collective-permute-start.7 = (f32[2,128,128]{2,1,0:T(8,128)S(1)}, f32[2,128,128]{2,1,0:T(8,128)S(1)}, u32[]{:S(2)}, u32[]{:S(2)}) collective-permute-start(f32[2,128,128]{2,1,0:T(8,128)S(1)} %get-tuple-element.21), channel_id=1, source_target_pairs={{0,8},{8,0},{16,24},{24,16},{1,9},{9,1},{17,25},{25,17},{2,10},{10... | collective-permute-start | bytes 393224 | tf_op jit(solution)/shard_map/ppermute | solution.py:315
  42.6 1.2 %collective-permute-start.8 = (f32[128,128]{1,0:T(8,128)S(1)}, f32[128,128]{1,0:T(8,128)S(1)}, u32[]{:S(2)}, u32[]{:S(2)}) collective-permute-start(f32[128,128]{1,0:T(8,128)S(1)} %get-tuple-element.22), channel_id=1, source_target_pairs={{0,1},{1,0},{2,3},{3,2},{4,5},{5,4},{6,7},{7,6},{8,9},{9,8},{10,11... | collective-permute-start | bytes 196616 | tf_op jit(solution)/shard_map/ppermute | solution.py:316
  43.8 0.1 collective-permute-start.9
  43.8 2.1 %collective-permute-done.8.refs_1_ = f32[128,128]{1,0:T(8,128)S(1)} collective-permute-done((f32[128,128]{1,0:T(8,128)S(1)}, f32[128,128]{1,0:T(8,128)S(1)}, u32[]{:S(2)}, u32[]{:S(2)}) %collective-permute-start.8) | collective-permute-done | bytes 65568 | tf_op jit(solution)/shard_map/ppermute | solution.py:316
  46.0 2.5 %collective-permute-done.9.refs_2_ = f32[128,128]{1,0:T(8,128)S(1)} collective-permute-done((f32[128,128]{1,0:T(8,128)S(1)}, f32[128,128]{1,0:T(8,128)S(1)}, u32[]{:S(2)}, u32[]{:S(2)}) %collective-permute-start.9) | collective-permute-done | bytes 65568 | tf_op jit(solution)/shard_map/ppermute | solution.py:320
  48.4 0.0 collective-permute-done.7.other_ref
  48.4 0.7 %shard_map.58 = (f32[2,128,128]{2,1,0:T(8,128)S(1)}, f32[2,64,128]{2,1,0:T(8,128)S(1)}, f32[2,64,128]{2,1,0:T(8,128)S(1)}) custom-call(s32[2]{0:T(128)S(1)} %bitcast.8, f32[2,128,128]{2,1,0:T(8,128)S(1)} %get-tuple-element.20.mine_ref, f32[2,128,128]{2,1,0:T(8,128)S(1)} %collective-permute-done.7.other_ref, s32[2]{0:T(128)S(1)} %collective-permute-done.2.refs_0_, ...), custom_call_target="tpu_custom_call" | custom-call | tf_op jit(solution)/shard_map/pallas_call | solution.py:245
  49.1 6.0 %collective-permute-start.10 = (f32[2,64,128]{2,1,0:T(8,128)S(1)}, f32[2,64,128]{2,1,0:T(8,128)S(1)}, u32[]{:S(2)}, u32[]{:S(2)}) collective-permute-start(f32[2,64,128]{2,1,0:T(8,128)S(1)} %get-tuple-element.25), channel_id=1, source_target_pairs={{0,2},{2,4},{4,6},{1,3},{3,5},{5,7},{8,10},{10,12},{12,14},{9,11},... | collective-permute-start | bytes 196616 | tf_op jit(solution)/shard_map/ppermute | solution.py:329
  55.1 1.9 %collective-permute-start.11 = (f32[2,64,128]{2,1,0:T(8,128)S(1)}, f32[2,64,128]{2,1,0:T(8,128)S(1)}, u32[]{:S(2)}, u32[]{:S(2)}) collective-permute-start(f32[2,64,128]{2,1,0:T(8,128)S(1)} %get-tuple-element.26), channel_id=1, source_target_pairs={{2,0},{4,2},{6,4},{3,1},{5,3},{7,5},{10,8},{12,10},{14,12},{11,9},... | collective-permute-start | bytes 196616 | tf_op jit(solution)/shard_map/ppermute | solution.py:328
  57.1 0.0 collective-permute-done.10
  57.1 3.6 %collective-permute-done.11 = f32[2,64,128]{2,1,0:T(8,128)S(1)} collective-permute-done((f32[2,64,128]{2,1,0:T(8,128)S(1)}, f32[2,64,128]{2,1,0:T(8,128)S(1)}, u32[]{:S(2)}, u32[]{:S(2)}) %collective-permute-start.11) | collective-permute-done | bytes 65568 | tf_op jit(solution)/shard_map/ppermute | solution.py:328
  60.7 0.7 %fusion = f32[1,2,128,128]{3,2,1,0:T(8,128)} fusion(f32[2,128,128]{2,1,0:T(8,128)S(1)} %get-tuple-element.24, f32[2,64,128]{2,1,0:T(8,128)S(1)} %collective-permute-done.11, f32[2,64,128]{2,1,0:T(8,128)S(1)} %collective-permute-done.10), kind=kLoop, calls=%fused_computation.1 | loop fusion | flops 65536 | bytes 393216 | tf_op jit(solution)/shard_map/broadcast_in_dim | solution.py:330
Async XLA Ops:
  0.0 25.7 %copy-start.1 = (bf16[8,256,256]{2,1,0:T(8,128)(2,1)S(1)}, bf16[8,256,256]{2,1,0:T(8,128)(2,1)}, u32[]{:S(2)}) copy-start(bf16[8,256,256]{2,1,0:T(8,128)(2,1)} %constant.17.clone.table_ref) | copy-start | bytes 3145732
  0.0 25.7 %copy-start.2 = (f32[4,2,128,128]{3,2,1,0:T(8,128)S(1)}, f32[4,2,128,128]{3,2,1,0:T(8,128)}, u32[]{:S(2)}) copy-start(f32[4,2,128,128]{3,2,1,0:T(8,128)} %refs_0_.1) | copy-start | bytes 1572868
  1.1 12.5 %collective-permute-start.4 = (f32[2,2,128,128]{3,2,1,0:T(8,128)S(1)}, f32[2,2,128,128]{3,2,1,0:T(8,128)S(1)}, u32[]{:S(2)}, u32[]{:S(2)}) collective-permute-start(f32[2,2,128,128]{3,2,1,0:T(8,128)S(1)} %constant_dynamic-slice_fusion), channel_id=1, source_target_pairs={{0,24},{8,16},{16,8},{24,0},{1,25},{9,17},{17,9},{25,1},{2,26},{10... | collective-permute-start | bytes 786440 | tf_op jit(solution)/shard_map/ppermute | solution.py:277
  6.4 8.5 %collective-permute-start.1 = (f32[4,2,64,128]{3,2,1,0:T(8,128)S(1)}, f32[4,2,64,128]{3,2,1,0:T(8,128)S(1)}, u32[]{:S(2)}, u32[]{:S(2)}) collective-permute-start(f32[4,2,64,128]{3,2,1,0:T(8,128)S(1)} %get-tuple-element.27), channel_id=1, source_target_pairs={{2,0},{4,2},{6,4},{3,1},{5,3},{7,5},{10,8},{12,10},{14,12},{11,9},... | collective-permute-start | bytes 786440 | tf_op jit(solution)/shard_map/ppermute | solution.py:273
  9.3 6.3 %collective-permute-start = (f32[4,2,64,128]{3,2,1,0:T(8,128)S(1)}, f32[4,2,64,128]{3,2,1,0:T(8,128)S(1)}, u32[]{:S(2)}, u32[]{:S(2)}) collective-permute-start(f32[4,2,64,128]{3,2,1,0:T(8,128)S(1)} %get-tuple-element.28), channel_id=1, source_target_pairs={{0,2},{2,4},{4,6},{1,3},{3,5},{5,7},{8,10},{10,12},{12,14},{9,11},... | collective-permute-start | bytes 786440 | tf_op jit(solution)/shard_map/ppermute | solution.py:272
  12.3 2.6 %collective-permute-start.2 = (s32[2]{0:T(128)}, s32[2]{0:T(128)S(1)}, u32[]{:S(2)}, u32[]{:S(2)}) collective-permute-start(s32[2]{0:T(128)} %bitcast.5), channel_id=1, source_target_pairs={{0,1},{1,0},{2,3},{3,2},{4,5},{5,4},{6,7},{7,6},{8,9},{9,8},{10,11... | collective-permute-start | bytes 32 | tf_op jit(solution)/shard_map/ppermute | solution.py:274
  13.6 5.2 %collective-permute-start.5 = (f32[2,2,128,128]{3,2,1,0:T(8,128)S(1)}, f32[2,2,128,128]{3,2,1,0:T(8,128)S(1)}, u32[]{:S(2)}, u32[]{:S(2)}) collective-permute-start(f32[2,2,128,128]{3,2,1,0:T(8,128)S(1)} %collective-permute-done.4.refs_2_.refs_1_), channel_id=1, source_target_pairs={{0,2},{2,0},{4,6},{6,4},{1,3},{3,1},{5,7},{7,5},{8,10},{10,8},{12,... | collective-permute-start | bytes 786440 | tf_op jit(solution)/shard_map/ppermute | solution.py:279
  15.6 1.0 %copy-start = (f32[4,2,128,128]{3,2,1,0:T(8,128)S(1)}, f32[4,2,128,128]{3,2,1,0:T(8,128)}, u32[]{:S(2)}) copy-start(f32[4,2,128,128]{3,2,1,0:T(8,128)} %tile_ref.3) | copy-start | bytes 1572868
  16.6 18.0 %copy-start.3 = (f32[1,1,1,128,128]{4,3,2,1,0:T(8,128)S(1)}, f32[1,1,1,128,128]{4,3,2,1,0:T(8,128)}, u32[]{:S(2)}) copy-start(f32[1,1,1,128,128]{4,3,2,1,0:T(8,128)} %param.8) | copy-start | bytes 196612
  17.6 8.1 %collective-permute-start.3 = (f32[4,128,128]{2,1,0:T(8,128)S(1)}, f32[4,128,128]{2,1,0:T(8,128)S(1)}, u32[]{:S(2)}, u32[]{:S(2)}) collective-permute-start(f32[4,128,128]{2,1,0:T(8,128)S(1)} %shard_map.55), channel_id=1, source_target_pairs={{0,1},{1,0},{2,3},{3,2},{4,5},{5,4},{6,7},{7,6},{8,9},{9,8},{10,11... | collective-permute-start | bytes 786440 | tf_op jit(solution)/shard_map/ppermute | solution.py:290
  25.7 0.7 %copy-start.4 = (s32[1,1,1,2]{3,2,1,0:T(1,128)S(1)}, s32[1,1,1,2]{3,2,1,0:T(1,128)}, u32[]{:S(2)}) copy-start(s32[1,1,1,2]{3,2,1,0:T(1,128)} %param.7) | copy-start | bytes 28
  31.0 3.7 %collective-permute-start.6 = (f32[128,128]{1,0:T(8,128)S(1)}, f32[128,128]{1,0:T(8,128)S(1)}, u32[]{:S(2)}, u32[]{:S(2)}) collective-permute-start(f32[128,128]{1,0:T(8,128)S(1)} %get-tuple-element.16.mine_ref), channel_id=1, source_target_pairs={{0,8},{8,0},{16,24},{24,16},{1,9},{9,1},{17,25},{25,17},{2,10},{10... | collective-permute-start | bytes 196616 | tf_op jit(solution)/shard_map/ppermute | solution.py:307
  41.0 7.4 %collective-permute-start.7 = (f32[2,128,128]{2,1,0:T(8,128)S(1)}, f32[2,128,128]{2,1,0:T(8,128)S(1)}, u32[]{:S(2)}, u32[]{:S(2)}) collective-permute-start(f32[2,128,128]{2,1,0:T(8,128)S(1)} %get-tuple-element.21), channel_id=1, source_target_pairs={{0,8},{8,0},{16,24},{24,16},{1,9},{9,1},{17,25},{25,17},{2,10},{10... | collective-permute-start | bytes 393224 | tf_op jit(solution)/shard_map/ppermute | solution.py:315
  42.6 3.4 %collective-permute-start.8 = (f32[128,128]{1,0:T(8,128)S(1)}, f32[128,128]{1,0:T(8,128)S(1)}, u32[]{:S(2)}, u32[]{:S(2)}) collective-permute-start(f32[128,128]{1,0:T(8,128)S(1)} %get-tuple-element.22), channel_id=1, source_target_pairs={{0,1},{1,0},{2,3},{3,2},{4,5},{5,4},{6,7},{7,6},{8,9},{9,8},{10,11... | collective-permute-start | bytes 196616 | tf_op jit(solution)/shard_map/ppermute | solution.py:316
  43.8 4.7 %collective-permute-start.9 = (f32[128,128]{1,0:T(8,128)S(1)}, f32[128,128]{1,0:T(8,128)S(1)}, u32[]{:S(2)}, u32[]{:S(2)}) collective-permute-start(f32[128,128]{1,0:T(8,128)S(1)} %get-tuple-element.23), channel_id=1, source_target_pairs={{0,9},{1,8},{8,1},{9,0},{16,25},{17,24},{24,17},{25,16},{2,11},{3,... | collective-permute-start | bytes 196616 | tf_op jit(solution)/shard_map/ppermute | solution.py:320
  49.1 8.0 %collective-permute-start.10 = (f32[2,64,128]{2,1,0:T(8,128)S(1)}, f32[2,64,128]{2,1,0:T(8,128)S(1)}, u32[]{:S(2)}, u32[]{:S(2)}) collective-permute-start(f32[2,64,128]{2,1,0:T(8,128)S(1)} %get-tuple-element.25), channel_id=1, source_target_pairs={{0,2},{2,4},{4,6},{1,3},{3,5},{5,7},{8,10},{10,12},{12,14},{9,11},... | collective-permute-start | bytes 196616 | tf_op jit(solution)/shard_map/ppermute | solution.py:329
  55.1 5.6 %collective-permute-start.11 = (f32[2,64,128]{2,1,0:T(8,128)S(1)}, f32[2,64,128]{2,1,0:T(8,128)S(1)}, u32[]{:S(2)}, u32[]{:S(2)}) collective-permute-start(f32[2,64,128]{2,1,0:T(8,128)S(1)} %get-tuple-element.26), channel_id=1, source_target_pairs={{2,0},{4,2},{6,4},{3,1},{5,3},{7,5},{10,8},{12,10},{14,12},{11,9},... | collective-permute-start | bytes 196616 | tf_op jit(solution)/shard_map/ppermute | solution.py:328
where the time goes:
time: 61.7 us; the launch traced here: 61.4 us
  starting transfers between devices  25.4 us (41%)
  waiting for transfers between devices  18.7 us (30%)
  Pallas kernels  12.6 us (20%)
  local copies, waits for them, and re-layouts  3.86 us (6%)
  other arithmetic  0.67 us (1%)
    pallas_call x4, Pallas kernels, call(): pl.pallas_call(kernel, out_shape=outs, in_specs=[SMEM_SPEC if i in scalar...  12.6 us
    ppermute x2, waiting for transfers between devices, body(): lax.ppermute(block, 'tx', edges(parity))  8.96 us
    ppermute x1, starting transfers between devices, body(): from_above = lax.ppermute(down, 'ty', downward)  6.05 us
    ppermute x1, starting transfers between devices, body(): far_half = lax.ppermute(part, 'mode', mirror)  4.22 us
    ppermute x1, waiting for transfers between devices, body(): from_below = lax.ppermute(up, 'ty', upward)  3.65 us
    ppermute x1, starting transfers between devices, body(): above = lax.ppermute(object_slices[:, :, half:], 'ty', downward)  3.05 us
    ppermute x1, starting transfers between devices, body(): below = lax.ppermute(object_slices[:, :, :half], 'ty', upward)  2.86 us
    ppermute x2, starting transfers between devices, body(): lax.ppermute(block, 'tx', edges(parity))  2.49 us
  transfers between devices with their start and end apart: 12, of which 7 were waited for; matrix products, arithmetic and copies ran while one was open for 2% of the time, Pallas kernels for 1%

commit v1 on v0

v1 whole, which is shorter than its diff:
```python
import functools

import jax
import jax.numpy as jnp
import numpy as np
from jax import lax
from jax.experimental import pallas as pl
from jax.experimental.pallas import tpu as pltpu
from jax.sharding import PartitionSpec as P

FRESNEL_RATE = 0.3
F32, BF16 = jnp.float32, jnp.bfloat16
VMEM_LIMIT = 24 * 2**20
ROWS = 32
SHARES = 2
MOVE, MOVE_BACK, FOURIER, FOURIER_BACK = 0, 2, 4, 6


def pair(table):
    high = table.astype(jnp.bfloat16)
    return [high, (table - high.astype(np.float64)).astype(jnp.bfloat16)]


def tables(length):
    counter = np.arange(length)
    fourier = np.exp(-2j * np.pi / length * (np.outer(counter, counter) % length)) / np.sqrt(length)
    frequency = np.where(counter < length // 2, counter, counter - length).astype(np.float64)
    chirp = np.exp(-1j * FRESNEL_RATE * frequency**2 / length)
    moved = fourier.conj() @ (chirp[:, None] * fourier)
    stacked = []
    for matrix in (moved, fourier):
        right = np.block([[matrix.real, matrix.imag], [-matrix.imag, matrix.real]])
        stacked += pair(right) + pair(right.T)
    return np.stack(stacked)


def dot(left, right):
    return jnp.dot(left, right, preferred_element_type=F32)


def split(value):
    high = value.astype(BF16)
    return high, (value - high.astype(F32)).astype(BF16)


def one_side(real, imag, table_ref, base):
    high, low = split(jnp.concatenate([real, imag], 1))
    both = dot(high, table_ref[base]) + dot(low, table_ref[base]) + dot(high, table_ref[base + 1])
    det = real.shape[1]
    return both[:, :det], both[:, det:]


def two_sided(real, imag, table_ref, base):
    upper_real, upper_imag = one_side(real, imag, table_ref, base)
    return one_side(upper_real.T, upper_imag.T, table_ref, base)


def iota(shape, dim):
    return lax.broadcasted_iota(jnp.int32, shape, dim)


def half_roll(plane):
    return pltpu.roll(plane, plane.shape[1] // 2, 1)


def is_right(index, parity):
    return lax.rem(index, 2) == parity


def has_partner(axis, parity):
    index = lax.axis_index(axis)
    first = index - lax.rem(index + parity, 2)
    return (first >= 0) & (first + 1 < lax.axis_size(axis))


def scalar(ref, *index):
    return jnp.max(ref[index])


def window_rows(above, tile, below, start):
    det = tile.shape[0]
    half = det // 2
    first = jnp.concatenate([above, tile[:half]], 0)
    second = jnp.concatenate([tile[half:], below], 0)
    mixed = jnp.where(iota(first.shape, 0) >= start, first, second)
    return pltpu.roll(mixed, lax.rem(det - start, det), 0)


def half_rows(ref_slice, row_parity, edge):
    half = ref_slice // 2
    return pl.multiple_of(jnp.where(row_parity == edge, half, 0), half)


def start_kernel(parities, row_axis, column_axis, place_hbm, tile_hbm, probe_hbm, *refs):
    count = len(parities)
    place_ref, tile_ref, part_ref, refs = refs[0], refs[1], refs[2], refs[3:]
    edge_refs, message_refs, place_smem, sems = refs[:2], refs[2 : 2 + count], refs[2 + count], refs[3 + count]
    slices, _, det, _ = tile_ref.shape
    share = part_ref.shape[0]
    row = lax.axis_index(row_axis)
    row_parity = lax.rem(row, 2)
    column = lax.axis_index(column_axis)
    whole = [pltpu.make_async_copy(tile_hbm.at[s], tile_ref.at[s], sems.at[s]) for s in range(slices)]
    sources = [(probe_hbm.at[pl.ds(lax.rem(row, SHARES) * share, share)], part_ref)]
    for edge, edge_ref in enumerate(edge_refs):
        first = half_rows(det, row_parity, edge)
        sources.append((tile_hbm.at[:, :, pl.ds(first, det // 2)], edge_ref))
    sources.append((place_hbm, place_smem))
    others = [pltpu.make_async_copy(*ends, sems.at[slices + i]) for i, ends in enumerate(sources)]
    for move in whole + others:
        move.start()
    lower = iota((det, det), 1) < det // 2
    for s in range(slices):
        whole[s].wait()
        for parity, message_ref in zip(parities, message_refs):
            right = is_right(column, parity)
            real, imag = tile_ref[s, 0], tile_ref[s, 1]
            to_right = jnp.where(lower, half_roll(real), imag)
            to_left = jnp.where(lower, real, half_roll(imag))
            message_ref[s] = jnp.where(right, to_right, to_left)
    for move in others:
        move.wait()
    for dim in range(2):
        place_ref[dim] = jnp.full(place_ref.shape[1:], place_smem[dim], jnp.int32)


def corner_kernel(parities, row_axis, *refs):
    count = len(parities)
    message_refs, corner_refs = refs[:count], refs[count + 2 :]
    det = message_refs[0].shape[1]
    row_parity = lax.rem(lax.axis_index(row_axis), 2)
    for edge, corner_ref in enumerate(corner_refs):
        first = half_rows(det, row_parity, edge)
        for j, message_ref in enumerate(message_refs):
            corner_ref[j] = message_ref[:, pl.ds(first, det // 2)]


class Window:
    def __init__(self, parities, row_axis, column_axis, place_ref, tile_ref, *refs):
        count = len(parities)
        self.tile, self.edges, self.corners, self.messages = tile_ref, refs[:2], refs[2:4], refs[4 : 4 + count]
        self.even_row = lax.rem(lax.axis_index(row_axis), 2) == 0
        self.on_edge = [has_partner(row_axis, parity) for parity in range(2)]
        column = lax.axis_index(column_axis)
        self.across = [(has_partner(column_axis, parity), is_right(column, parity)) for parity in parities]
        self.row, self.col = scalar(place_ref, 0), scalar(place_ref, 1)

    def rows_of(self, pair_refs, index, middle):
        even, odd = [jnp.where(there, ref[index], 0.0) for there, ref in zip(self.on_edge, pair_refs)]
        above, below = jnp.where(self.even_row, odd, even), jnp.where(self.even_row, even, odd)
        return window_rows(above, middle, below, self.row)

    def store(self, s, window_ref):
        det = self.tile.shape[-1]
        lanes = iota((det, det), 1)
        lower, late = lanes < det // 2, lanes >= self.col
        messages = [self.rows_of(self.corners, (j, s), ref[s]) for j, ref in enumerate(self.messages)]
        for c in range(2):
            own = half_roll(self.rows_of(self.edges, (s, c), self.tile[s, c]))
            left, right = jnp.zeros_like(own), jnp.zeros_like(own)
            for (there, at_right), message in zip(self.across, messages):
                turned = half_roll(message)
                right = right + jnp.where(there & at_right, turned if c == 0 else message, 0.0)
                left = left + jnp.where(there & ~at_right, message if c == 0 else turned, 0.0)
            mixed = jnp.where(late, jnp.where(lower, left, own), jnp.where(lower, own, right))
            window = pltpu.roll(mixed, lax.rem(det - self.col, det), 1)
            window_ref[s, c] = window.T if s % 2 == 1 else window


def first_forward_kernel(parities, row_axis, column_axis, table_ref, probe_ref, *refs):
    window_ref, state_refs = refs[-4], refs[-3:]
    window = Window(parities, row_axis, column_axis, *refs[:-4])
    run_forward(window_ref, table_ref, [probe_ref], [], *state_refs, prepare=window.store)


def forward_kernel(probe_count, window_ref, table_ref, *refs):
    run_forward(window_ref, table_ref, refs[:probe_count], refs[probe_count:-3], *refs[-3:])


def run_forward(window_ref, table_ref, probe_refs, before_refs, wave_ref, far_ref, intensity_ref, prepare=None):
    slices, _, det, _ = window_ref.shape
    slots = [ref.at[j] for ref in probe_refs for j in range(ref.shape[0])]
    total = jnp.zeros((det, det), F32)
    for s in range(slices):
        if prepare is not None:
            prepare(s, window_ref)
        real, imag = window_ref[s, 0], window_ref[s, 1]
        last = s == slices - 1
        for mode, probe in enumerate(slots):
            source = probe if s == 0 else wave_ref.at[s - 1, mode]
            wave_real, wave_imag = source[0], source[1]
            leave_real = wave_real * real - wave_imag * imag
            leave_imag = wave_real * imag + wave_imag * real
            out_real, out_imag = two_sided(leave_real, leave_imag, table_ref, FOURIER if last else MOVE)
            target = far_ref.at[mode] if last else wave_ref.at[s, mode]
            target[0] = out_real
            target[1] = out_imag
            if last:
                total = total + (out_real * out_real + out_imag * out_imag)
    for before_ref in before_refs:
        total = total + before_ref[...]
    intensity_ref[...] = total


def backward_kernel(parities, parts, mode_axis, column_axis, place_ref, *refs):
    count = len(parities)
    measured_ref, mine_ref, other_ref, table_ref, window_ref = refs[count : count + 5]
    refs = refs[count + 5 :]
    probe_refs, refs = refs[: sum(parts)], refs[sum(parts) :]
    wave_refs, far_refs, refs = refs[: len(parts)], refs[len(parts) : 2 * len(parts)], refs[2 * len(parts) :]
    center_ref, send_ref = refs[:2]
    strip_refs, send_strip_refs = refs[2 : 2 + count], refs[2 + count : 2 + 2 * count]
    term_ref, back_ref = refs[2 + 2 * count :]
    slices, _, det, _ = window_ref.shape
    col = scalar(place_ref, 1)
    me = lax.axis_index(mode_axis)
    peer = me + 1 - 2 * lax.rem(me, 2)
    column = lax.axis_index(column_axis)
    probes = [ref.at[j] for ref in probe_refs for j in range(ref.shape[0])]
    slots = [(k, j) for k, ref in enumerate(far_refs) for j in range(ref.shape[0])]
    intensity = mine_ref[...] + other_ref[...]
    weight = 1.0 - measured_ref[...] / jnp.maximum(jnp.sqrt(intensity), 1.0)
    for s in reversed(range(slices)):
        last = s == slices - 1
        now, before = s % 2, (s + 1) % 2
        if not last:
            real, imag = window_ref[s + 1, 0], window_ref[s + 1, 1]
        for mode, (k, j) in enumerate(slots):
            if last:
                pulled_real, pulled_imag = weight * far_refs[k][j, 0], weight * far_refs[k][j, 1]
            else:
                back_real, back_imag = back_ref[before, mode, 0], back_ref[before, mode, 1]
                pulled_real = real * back_real + imag * back_imag
                pulled_imag = real * back_imag - imag * back_real
            base = FOURIER_BACK if last else MOVE_BACK
            back_real, back_imag = two_sided(pulled_real, pulled_imag, table_ref, base)
            back_ref[now, mode, 0] = back_real
            back_ref[now, mode, 1] = back_imag
        for first in range(0, det, ROWS):
            rows = slice(first, first + ROWS)
            term_real, term_imag = jnp.zeros((ROWS, det), F32), jnp.zeros((ROWS, det), F32)
            for mode, (k, j) in enumerate(slots):
                wave = wave_refs[k].at[s - 1, j] if s > 0 else probes[mode]
                wave_real, wave_imag = wave[0, rows], wave[1, rows]
                back_real, back_imag = back_ref[now, mode, 0, rows], back_ref[now, mode, 1, rows]
                term_real = term_real + (wave_real * back_real + wave_imag * back_imag)
                term_imag = term_imag + (wave_real * back_imag - wave_imag * back_real)
            term_ref[s, 0, rows] = term_real
            term_ref[s, 1, rows] = term_imag
        if s % 2 == 1:
            for c in range(2):
                term_ref[s, c] = term_ref[s, c].T

    lanes = iota((det, det), 1)
    lower, late = lanes < det // 2, lanes >= col
    forth_shift = lax.rem(col, det)
    for owner, middle_ref, out_strip_refs in ((me, center_ref, strip_refs), (peer, send_ref, send_strip_refs)):
        early, latter = [], []
        for c in range(2):
            turned = pltpu.roll(term_ref[owner, c], forth_shift, 1)
            early.append(jnp.where(late, turned, 0.0))
            latter.append(jnp.where(late, 0.0, turned))
            middle_ref[c] = half_roll(jnp.where(lower, latter[c], early[c]))
        to_right = jnp.where(lower, half_roll(latter[0]), latter[1])
        to_left = jnp.where(lower, early[0], half_roll(early[1]))
        for parity, strip_ref in zip(parities, out_strip_refs):
            strip_ref[...] = jnp.where(is_right(column, parity), to_right, to_left)


def place_kernel(parities, row_axis, column_axis, place_ref, mine_ref, other_ref, *refs):
    count = len(parities)
    place_refs, one_refs, two_refs = refs[:count], refs[count : 2 * count], refs[2 * count : 3 * count]
    middle_ref, even_ref, odd_ref = refs[3 * count :]
    even_row = lax.rem(lax.axis_index(row_axis), 2) == 0
    det = mine_ref.shape[1]
    half = det // 2
    column = lax.axis_index(column_axis)
    rows, lower = iota((det, det), 0), iota((det, det), 1) < half
    start = scalar(place_ref, 0)

    def placed(plane, begin):
        turned = pltpu.roll(plane, lax.rem(begin, det), 0)
        late = rows >= begin
        return jnp.where(late, turned, 0.0), jnp.where(late, 0.0, turned)

    blocks = [list(placed(mine_ref[c] + other_ref[c], start)) for c in range(2)]
    for parity, partner_ref, one_ref, two_ref in zip(parities, place_refs, one_refs, two_refs):
        strip = jnp.where(has_partner(column_axis, parity), one_ref[...] + two_ref[...], 0.0)
        at_right = is_right(column, parity)
        for block, part in enumerate(placed(strip, scalar(partner_ref, 0))):
            turned = half_roll(part)
            real = jnp.where(lower != at_right, jnp.where(at_right, turned, part), 0.0)
            imag = jnp.where(lower != at_right, jnp.where(at_right, part, turned), 0.0)
            blocks[0][block] = blocks[0][block] + real
            blocks[1][block] = blocks[1][block] + imag
    for c in range(2):
        first, second = blocks[c]
        middle_ref[c, :half] = first[half:]
        middle_ref[c, half:] = second[:half]
        even_ref[c] = jnp.where(even_row, second[half:], first[:half])
        odd_ref[c] = jnp.where(even_row, first[:half], second[half:])


HBM_SPEC = pl.BlockSpec(memory_space=pltpu.HBM)
VMEM_SPEC = pl.BlockSpec(memory_space=pltpu.VMEM)


def call(kernel, outs, operands, scratch=(), in_spec=VMEM_SPEC):
    return pl.pallas_call(
        kernel,
        out_shape=outs,
        in_specs=[in_spec] * len(operands),
        out_specs=[VMEM_SPEC] * len(outs),
        scratch_shapes=scratch,
        compiler_params=pltpu.CompilerParams(vmem_limit_bytes=VMEM_LIMIT),
    )(*operands)


def body(object_slices, probe_modes, positions, measured):
    modes_here, _, det, _ = probe_modes.shape
    slices, half = object_slices.shape[0], det // 2
    groups, height, width = lax.axis_size("mode"), lax.axis_size("ty"), lax.axis_size("tx")

    def edges(size, parity):
        ends = [(i, (i + 1) % size) for i in range(parity, size, 2)]
        return ends + [(j, i) for i, j in ends]

    parities = (0,) if width == 2 else (0, 1)
    count = len(parities)
    mirror = [(i, groups - 1 - i) for i in range(groups)]
    neighbour = edges(groups, 0)

    def shape(*sizes):
        return jax.ShapeDtypeStruct(sizes, F32)

    place, tile, part, even, odd, *messages = call(
        functools.partial(start_kernel, parities, "ty", "tx"),
        [
            jax.ShapeDtypeStruct((2, 8, 128), jnp.int32),
            shape(*object_slices.shape),
            shape(modes_here // SHARES, 2, det, det),
            shape(slices, 2, half, det),
            shape(slices, 2, half, det),
        ]
        + [shape(slices, det, det)] * count,
        [pltpu.with_memory_space_constraint(x, pltpu.HBM) for x in (positions.reshape(2), object_slices, probe_modes)],
        scratch=[pltpu.SMEM((2,), jnp.int32), pltpu.SemaphoreType.DMA((slices + 4,))],
        in_spec=HBM_SPEC,
    )
    fetched = lax.ppermute(part, "mode", mirror)
    messages = [lax.ppermute(block, "tx", edges(width, parity)) for parity, block in zip(parities, messages)]
    borders = [lax.ppermute(block, "ty", edges(height, edge)) for edge, block in enumerate((even, odd))]
    corners = call(
        functools.partial(corner_kernel, parities, "ty"),
        [shape(count, slices, half, det)] * 2,
        [*messages, *borders],
    )
    corners = [lax.ppermute(block, "ty", edges(height, edge)) for edge, block in enumerate(corners)]
    fetched, *_ = lax.optimization_barrier((fetched, *corners))
    fetched = [fetched, lax.ppermute(fetched, "ty", edges(height, 0))]

    table = jnp.asarray(tables(det))

    def states(modes):
        return [shape(slices - 1, modes, 2, det, det), shape(modes, 2, det, det), shape(det, det)]

    window, wave, far, mine = call(
        functools.partial(first_forward_kernel, parities, "ty", "tx"),
        [shape(slices, 2, det, det)] + states(modes_here),
        [table, probe_modes, place, tile, *borders, *corners, *messages],
    )
    more_wave, more_far, mine = call(
        functools.partial(forward_kernel, SHARES), states(modes_here), [window, table, *fetched, mine]
    )
    other = lax.ppermute(mine, "mode", neighbour)
    place, _ = lax.optimization_barrier((place, mine))
    partner_places = [lax.ppermute(place, "tx", edges(width, parity)) for parity in parities]
    amplitudes = measured.reshape(det, det)
    center, send, *strips = call(
        functools.partial(backward_kernel, parities, (1, SHARES), "mode", "tx"),
        [shape(2, det, det)] * 2 + [shape(det, det)] * (2 * count),
        [place, *partner_places, amplitudes if slices % 2 == 0 else amplitudes.T, mine, other]
        + [table, window, probe_modes, *fetched, wave, more_wave, far, more_far],
        scratch=[pltpu.VMEM((slices, 2, det, det), F32), pltpu.VMEM((2, 2 * modes_here, 2, det, det), F32)],
    )
    received = lax.ppermute(send, "mode", neighbour)
    ones = [lax.ppermute(block, "tx", edges(width, parity)) for parity, block in zip(parities, strips[:count])]
    twos = []
    for parity, block in zip(parities, strips[count:]):
        route = [(i * width + p, j * width + q) for i, j in neighbour for p, q in edges(width, parity)]
        twos.append(lax.ppermute(block, ("mode", "tx"), route))
    middle, even, odd = call(
        functools.partial(place_kernel, parities, "ty", "tx"),
        [shape(2, det, det), shape(2, half, det), shape(2, half, det)],
        [place, center, received, *partner_places, *ones, *twos],
    )
    even, odd = [
        jnp.where(has_partner("ty", edge), lax.ppermute(block, "ty", edges(height, edge)), 0.0)
        for edge, block in enumerate((even, odd))
    ]
    even_row = lax.rem(lax.axis_index("ty"), 2) == 0
    border = jnp.concatenate([jnp.where(even_row, odd, even), jnp.where(even_row, even, odd)], 1)
    return (middle + border)[None]


def solution(mesh):
    return jax.shard_map(
        body,
        mesh=mesh,
        in_specs=(
            P(None, None, "ty", "tx"),
            P("mode", None, None, None),
            P("ty", "tx", None, None),
            P("ty", "tx", None, None, None),
        ),
        out_specs=P("mode", None, "ty", "tx"),
        check_vma=False,
    )
```

time: 61.7 us -> 46.3 us (0.75)
  the two profiles are of different devices: /device:TPU:1 before, /device:TPU:0 now
where the time goes in v1:
time: 46.3 us; the launch traced here: 46.1 us
  waiting for transfers between devices  17.2 us (37%)
  starting transfers between devices  16.7 us (36%)
  Pallas kernels  11.4 us (25%)
  other arithmetic  0.69 us (1%)
    pallas_call x6, Pallas kernels, call(): pl.pallas_call(kernel, out_shape=outs, in_specs=[in_spec] * len(operands)...  11.4 us
    ppermute x6, waiting for transfers between devices, body(): lax.ppermute(block, 'ty', edges(height, edge))  6.78 us
    ppermute x6, starting transfers between devices, body(): lax.ppermute(block, 'ty', edges(height, edge))  4.34 us
    ppermute x2, waiting for transfers between devices, body(): lax.ppermute(block, 'tx', edges(width, parity))  3.78 us
    ppermute x1, starting transfers between devices, body(): fetched = lax.ppermute(part, 'mode', mirror)  3.6 us
    ppermute x1, waiting for transfers between devices, body(): lax.ppermute(place, 'tx', edges(width, parity))  3.04 us
    ppermute x1, starting transfers between devices, body(): other = lax.ppermute(mine, 'mode', neighbour)  2.72 us
    ppermute x1, waiting for transfers between devices, body(): fetched = lax.ppermute(part, 'mode', mirror)  2.64 us
  transfers between devices with their start and end apart: 14, of which 8 were waited for; matrix products, arithmetic and copies ran while one was open for 0% of the time, Pallas kernels for 6%

profile of v1, /device:TPU:0, one launch (start us, length us, event | category | flops | bytes accessed | tf_op | source)
XLA Modules:
  0.0 46.1 jit_solution(13121854777196521770)
XLA Ops:
  0.0 0.0 copy-start
  0.0 0.0 copy-start.1
  0.0 1.6 %shard_map.55 = (s32[2,8,128]{2,1,0:T(8,128)S(1)}, f32[4,2,128,128]{3,2,1,0:T(8,128)S(1)}, f32[2,2,128,128]{3,2,1,0:T(8,128)S(1)}, f32[4,2,64,128]{3,2,1,0:T(8,1...) custom-call(s32[2]{0:T(128)} %bitcast.5, f32[4,2,128,128]{3,2,1,0:T(8,128)} %tile_hbm.1, ...), custom_call_target="tpu_custom_call" | custom-call | tf_op jit(solution)/shard_map/pallas_call | solution.py:309
  1.6 0.5 %collective-permute-start = (f32[4,2,64,128]{3,2,1,0:T(8,128)S(1)}, f32[4,2,64,128]{3,2,1,0:T(8,128)S(1)}, u32[]{:S(2)}, u32[]{:S(2)}) collective-permute-start(f32[4,2,64,128]{3,2,1,0:T(8,128)S(1)} %get-tuple-element.31), channel_id=1, source_target_pairs={{0,2},{4,6},{2,0},{6,4},{1,3},{5,7},{3,1},{7,5},{8,10},{12,14},{10... | collective-permute-start | bytes 786440 | tf_op jit(solution)/shard_map/ppermute | solution.py:352
  2.1 2.6 %collective-permute-start.1 = (f32[4,2,64,128]{3,2,1,0:T(8,128)S(1)}, f32[4,2,64,128]{3,2,1,0:T(8,128)S(1)}, u32[]{:S(2)}, u32[]{:S(2)}) collective-permute-start(f32[4,2,64,128]{3,2,1,0:T(8,128)S(1)} %get-tuple-element.32), channel_id=1, source_target_pairs={{2,4},{6,0},{4,2},{0,6},{3,5},{7,1},{5,3},{1,7},{10,12},{14,8},{12... | collective-permute-start | bytes 786440 | tf_op jit(solution)/shard_map/ppermute | solution.py:352
  4.7 1.5 %collective-permute-start.2 = (f32[4,128,128]{2,1,0:T(8,128)S(1)}, f32[4,128,128]{2,1,0:T(8,128)S(1)}, u32[]{:S(2)}, u32[]{:S(2)}) collective-permute-start(f32[4,128,128]{2,1,0:T(8,128)S(1)} %get-tuple-element.33), channel_id=1, source_target_pairs={{0,1},{1,0},{2,3},{3,2},{4,5},{5,4},{6,7},{7,6},{8,9},{9,8},{10,11... | collective-permute-start | bytes 786440 | tf_op jit(solution)/shard_map/ppermute | solution.py:351
  6.2 3.6 %collective-permute-start.5 = (f32[2,2,128,128]{3,2,1,0:T(8,128)S(1)}, f32[2,2,128,128]{3,2,1,0:T(8,128)S(1)}, u32[]{:S(2)}, u32[]{:S(2)}) collective-permute-start(f32[2,2,128,128]{3,2,1,0:T(8,128)S(1)} %get-tuple-element.37), channel_id=1, source_target_pairs={{0,24},{8,16},{16,8},{24,0},{1,25},{9,17},{17,9},{25,1},{2,26},{10... | collective-permute-start | bytes 786440 | tf_op jit(solution)/shard_map/ppermute | solution.py:350
  9.8 0.0 collective-permute-done.refs_1_.refs_2_
  9.8 1.5 %collective-permute-done.1.refs_2_.refs_3_ = f32[4,2,64,128]{3,2,1,0:T(8,128)S(1)} collective-permute-done((f32[4,2,64,128]{3,2,1,0:T(8,128)S(1)}, f32[4,2,64,128]{3,2,1,0:T(8,128)S(1)}, u32[]{:S(2)}, u32[]{:S(2)}) %collective-permute-start.1) | collective-permute-done | bytes 262176 | tf_op jit(solution)/shard_map/ppermute | solution.py:352
  11.3 1.7 %collective-permute-done.2.refs_0_.refs_6_ = f32[4,128,128]{2,1,0:T(8,128)S(1)} collective-permute-done((f32[4,128,128]{2,1,0:T(8,128)S(1)}, f32[4,128,128]{2,1,0:T(8,128)S(1)}, u32[]{:S(2)}, u32[]{:S(2)}) %collective-permute-start.2) | collective-permute-done | bytes 262176 | tf_op jit(solution)/shard_map/ppermute | solution.py:351
  13.0 0.1 collective-permute-start.3
  13.1 0.4 collective-permute-start.4
  13.5 2.6 %collective-permute-done.5.refs_0_.refs_7_ = f32[2,2,128,128]{3,2,1,0:T(8,128)S(1)} collective-permute-done((f32[2,2,128,128]{3,2,1,0:T(8,128)S(1)}, f32[2,2,128,128]{3,2,1,0:T(8,128)S(1)}, u32[]{:S(2)}, u32[]{:S(2)}) %collective-permute-start.5) | collective-permute-done | bytes 262176 | tf_op jit(solution)/shard_map/ppermute | solution.py:350
  16.2 0.0 collective-permute-done.3.refs_4_
  16.2 2.2 %collective-permute-done.4.refs_5_ = f32[1,4,64,128]{3,2,1,0:T(8,128)S(1)} collective-permute-done((f32[1,4,64,128]{3,2,1,0:T(8,128)S(1)}, f32[1,4,64,128]{3,2,1,0:T(8,128)S(1)}, u32[]{:S(2)}, u32[]{:S(2)}) %collective-permute-start.4) | collective-permute-done | bytes 131104 | tf_op jit(solution)/shard_map/ppermute | solution.py:358
  18.4 0.4 collective-permute-start.6
  18.8 0.0 copy-done
  18.8 0.0 copy-done.1
  18.8 2.9 %shard_map.57 = (f32[4,2,128,128]{3,2,1,0:T(8,128)S(1)}, f32[3,4,2,128,128]{4,3,2,1,0:T(8,128)S(1)}, f32[4,2,128,128]{3,2,1,0:T(8,128)S(1)}, f32[128,128]{1,0:T(8,128)S(1)}) custom-call(bf16[8,256,256]{2,1,0:T(8,128)(2,1)S(1)} %copy-done, f32[4,2,128,128]{3,2,1,0:T(8,128)S(1)} %copy-done.1, s32[2,8,128]{2,1,0:T(8,128)S(1)} %get-tuple-element.41.refs_0_.place_ref, ...), custom_call_target="tpu_custom_call" | custom-call | tf_op jit(solution)/shard_map/pallas_call | solution.py:309
  21.7 0.0 copy-start.2
  21.7 0.0 collective-permute-done.6.refs_1_.refs_8_
  21.7 2.2 %shard_map.58 = (f32[3,4,2,128,128]{4,3,2,1,0:T(8,128)S(1)}, f32[4,2,128,128]{3,2,1,0:T(8,128)S(1)}, f32[128,128]{1,0:T(8,128)S(1)}) custom-call(f32[4,2,128,128]{3,2,1,0:T(8,128)S(1)} %get-tuple-element.36.window_ref.refs_5_, bf16[8,256,256]{2,1,0:T(8,128)(2,1)S(1)} %copy-done, f32[2,2,128,128]{3,2,1,0:T(8,128)S(1)} %collective-permute-done.5.refs_0_.refs_7_, ...), custom_call_target="tpu_custom_call" | custom-call | tf_op jit(solution)/shard_map/pallas_call | solution.py:309
  23.9 2.7 %collective-permute-start.8 = (f32[128,128]{1,0:T(8,128)S(1)}, f32[128,128]{1,0:T(8,128)S(1)}, u32[]{:S(2)}, u32[]{:S(2)}) collective-permute-start(f32[128,128]{1,0:T(8,128)S(1)} %get-tuple-element.40.refs_2_), channel_id=1, source_target_pairs={{0,8},{16,24},{8,0},{24,16},{1,9},{17,25},{9,1},{25,17},{2,10},{18... | collective-permute-start | bytes 196616 | tf_op jit(solution)/shard_map/ppermute | solution.py:375
  26.7 0.6 %collective-permute-start.7 = (s32[2,8,128]{2,1,0:T(8,128)S(1)}, s32[2,8,128]{2,1,0:T(8,128)S(1)}, u32[]{:S(2)}, u32[]{:S(2)}) collective-permute-start(s32[2,8,128]{2,1,0:T(8,128)S(1)} %get-tuple-element.41.refs_0_.place_ref), channel_id=1, source_target_pairs={{0,1},{1,0},{2,3},{3,2},{4,5},{5,4},{6,7},{7,6},{8,9},{9,8},{10,11... | collective-permute-start | bytes 24584 | tf_op jit(solution)/shard_map/ppermute | solution.py:377
  27.3 3.0 %collective-permute-done.7.refs_0_ = s32[2,8,128]{2,1,0:T(8,128)S(1)} collective-permute-done((s32[2,8,128]{2,1,0:T(8,128)S(1)}, s32[2,8,128]{2,1,0:T(8,128)S(1)}, u32[]{:S(2)}, u32[]{:S(2)}) %collective-permute-start.7) | collective-permute-done | bytes 8224 | tf_op jit(solution)/shard_map/ppermute | solution.py:377
  30.3 0.0 collective-permute-done.8.refs_3_
  30.3 0.0 copy-done.2
  30.3 4.4 %shard_map.59 = (f32[2,128,128]{2,1,0:T(8,128)S(1)}, f32[2,128,128]{2,1,0:T(8,128)S(1)}, f32[128,128]{1,0:T(8,128)S(1)}, f32[128,128]{1,0:T(8,128)S(1)}) custom-call(s32[2,8,128]{2,1,0:T(8,128)S(1)} %get-tuple-element.41.refs_0_.place_ref, s32[2,8,128]{2,1,0:T(8,128)S(1)} %collective-permute-done.7.refs_0_, f32[128,128]{1,0:T(8,128)S(1)} %bitcast.4, ...), custom_call_target="tpu_custom_call" | custom-call | tf_op jit(solution)/shard_map/pallas_call | solution.py:309
  34.7 0.9 %collective-permute-start.9 = (f32[2,128,128]{2,1,0:T(8,128)S(1)}, f32[2,128,128]{2,1,0:T(8,128)S(1)}, u32[]{:S(2)}, u32[]{:S(2)}) collective-permute-start(f32[2,128,128]{2,1,0:T(8,128)S(1)} %get-tuple-element.47), channel_id=1, source_target_pairs={{0,8},{16,24},{8,0},{24,16},{1,9},{17,25},{9,1},{25,17},{2,10},{18... | collective-permute-start | bytes 393224 | tf_op jit(solution)/shard_map/ppermute | solution.py:386
  35.6 0.6 %collective-permute-start.10 = (f32[128,128]{1,0:T(8,128)S(1)}, f32[128,128]{1,0:T(8,128)S(1)}, u32[]{:S(2)}, u32[]{:S(2)}) collective-permute-start(f32[128,128]{1,0:T(8,128)S(1)} %get-tuple-element.48), channel_id=1, source_target_pairs={{0,1},{1,0},{2,3},{3,2},{4,5},{5,4},{6,7},{7,6},{8,9},{9,8},{10,11... | collective-permute-start | bytes 196616 | tf_op jit(solution)/shard_map/ppermute | solution.py:387
  36.1 2.1 %collective-permute-start.11 = (f32[128,128]{1,0:T(8,128)S(1)}, f32[128,128]{1,0:T(8,128)S(1)}, u32[]{:S(2)}, u32[]{:S(2)}) collective-permute-start(f32[128,128]{1,0:T(8,128)S(1)} %get-tuple-element.49), channel_id=1, source_target_pairs={{0,9},{1,8},{16,25},{17,24},{8,1},{9,0},{24,17},{25,16},{2,11},{3,... | collective-permute-start | bytes 196616 | tf_op jit(solution)/shard_map/ppermute | solution.py:391
  38.2 2.1 %collective-permute-done.10.refs_1_ = f32[128,128]{1,0:T(8,128)S(1)} collective-permute-done((f32[128,128]{1,0:T(8,128)S(1)}, f32[128,128]{1,0:T(8,128)S(1)}, u32[]{:S(2)}, u32[]{:S(2)}) %collective-permute-start.10) | collective-permute-done | bytes 65568 | tf_op jit(solution)/shard_map/ppermute | solution.py:387
  40.3 1.0 %collective-permute-done.11.refs_2_ = f32[128,128]{1,0:T(8,128)S(1)} collective-permute-done((f32[128,128]{1,0:T(8,128)S(1)}, f32[128,128]{1,0:T(8,128)S(1)}, u32[]{:S(2)}, u32[]{:S(2)}) %collective-permute-start.11) | collective-permute-done | bytes 65568 | tf_op jit(solution)/shard_map/ppermute | solution.py:391
  41.3 0.0 collective-permute-done.9.other_ref
  41.3 0.3 shard_map.60
  41.7 0.1 collective-permute-start.12
  41.7 0.6 %collective-permute-start.13 = (f32[2,64,128]{2,1,0:T(8,128)S(1)}, f32[2,64,128]{2,1,0:T(8,128)S(1)}, u32[]{:S(2)}, u32[]{:S(2)}) collective-permute-start(f32[2,64,128]{2,1,0:T(8,128)S(1)} %get-tuple-element.52), channel_id=1, source_target_pairs={{0,2},{4,6},{2,0},{6,4},{1,3},{5,7},{3,1},{7,5},{8,10},{12,14},{10... | collective-permute-start | bytes 196616 | tf_op jit(solution)/shard_map/ppermute | solution.py:398
  42.3 3.1 %collective-permute-done.12 = f32[2,64,128]{2,1,0:T(8,128)S(1)} collective-permute-done((f32[2,64,128]{2,1,0:T(8,128)S(1)}, f32[2,64,128]{2,1,0:T(8,128)S(1)}, u32[]{:S(2)}, u32[]{:S(2)}) %collective-permute-start.12) | collective-permute-done | bytes 65568 | tf_op jit(solution)/shard_map/ppermute | solution.py:398
  45.4 0.0 collective-permute-done.13
  45.4 0.7 %fusion = f32[1,2,128,128]{3,2,1,0:T(8,128)} fusion(f32[2,128,128]{2,1,0:T(8,128)S(1)} %get-tuple-element.50, f32[2,64,128]{2,1,0:T(8,128)S(1)} %get-tuple-element.54, f32[2,64,128]{2,1,0:T(8,128)S(1)} %get-tuple-element.53), kind=kLoop, calls=%fused_computation.1 | loop fusion | flops 65536 | bytes 393216 | tf_op jit(solution)/shard_map/broadcast_in_dim | solution.py:403
  (2 shorter events, 0.0 us)
Async XLA Ops:
  0.0 18.8 %copy-start = (bf16[8,256,256]{2,1,0:T(8,128)(2,1)S(1)}, bf16[8,256,256]{2,1,0:T(8,128)(2,1)}, u32[]{:S(2)}) copy-start(bf16[8,256,256]{2,1,0:T(8,128)(2,1)} %constant.21.clone.table_ref.refs_4_) | copy-start | bytes 3145732
  0.0 18.8 %copy-start.1 = (f32[4,2,128,128]{3,2,1,0:T(8,128)S(1)}, f32[4,2,128,128]{3,2,1,0:T(8,128)}, u32[]{:S(2)}) copy-start(f32[4,2,128,128]{3,2,1,0:T(8,128)} %refs_6_.1) | copy-start | bytes 1572868
  1.6 8.3 %collective-permute-start = (f32[4,2,64,128]{3,2,1,0:T(8,128)S(1)}, f32[4,2,64,128]{3,2,1,0:T(8,128)S(1)}, u32[]{:S(2)}, u32[]{:S(2)}) collective-permute-start(f32[4,2,64,128]{3,2,1,0:T(8,128)S(1)} %get-tuple-element.31), channel_id=1, source_target_pairs={{0,2},{4,6},{2,0},{6,4},{1,3},{5,7},{3,1},{7,5},{8,10},{12,14},{10... | collective-permute-start | bytes 786440 | tf_op jit(solution)/shard_map/ppermute | solution.py:352
  2.1 9.2 %collective-permute-start.1 = (f32[4,2,64,128]{3,2,1,0:T(8,128)S(1)}, f32[4,2,64,128]{3,2,1,0:T(8,128)S(1)}, u32[]{:S(2)}, u32[]{:S(2)}) collective-permute-start(f32[4,2,64,128]{3,2,1,0:T(8,128)S(1)} %get-tuple-element.32), channel_id=1, source_target_pairs={{2,4},{6,0},{4,2},{0,6},{3,5},{7,1},{5,3},{1,7},{10,12},{14,8},{12... | collective-permute-start | bytes 786440 | tf_op jit(solution)/shard_map/ppermute | solution.py:352
  4.7 8.3 %collective-permute-start.2 = (f32[4,128,128]{2,1,0:T(8,128)S(1)}, f32[4,128,128]{2,1,0:T(8,128)S(1)}, u32[]{:S(2)}, u32[]{:S(2)}) collective-permute-start(f32[4,128,128]{2,1,0:T(8,128)S(1)} %get-tuple-element.33), channel_id=1, source_target_pairs={{0,1},{1,0},{2,3},{3,2},{4,5},{5,4},{6,7},{7,6},{8,9},{9,8},{10,11... | collective-permute-start | bytes 786440 | tf_op jit(solution)/shard_map/ppermute | solution.py:351
  6.2 10.0 %collective-permute-start.5 = (f32[2,2,128,128]{3,2,1,0:T(8,128)S(1)}, f32[2,2,128,128]{3,2,1,0:T(8,128)S(1)}, u32[]{:S(2)}, u32[]{:S(2)}) collective-permute-start(f32[2,2,128,128]{3,2,1,0:T(8,128)S(1)} %get-tuple-element.37), channel_id=1, source_target_pairs={{0,24},{8,16},{16,8},{24,0},{1,25},{9,17},{17,9},{25,1},{2,26},{10... | collective-permute-start | bytes 786440 | tf_op jit(solution)/shard_map/ppermute | solution.py:350
  13.0 3.2 %collective-permute-start.3 = (f32[1,4,64,128]{3,2,1,0:T(8,128)S(1)}, f32[1,4,64,128]{3,2,1,0:T(8,128)S(1)}, u32[]{:S(2)}, u32[]{:S(2)}) collective-permute-start(f32[1,4,64,128]{3,2,1,0:T(8,128)S(1)} %get-tuple-element.34), channel_id=1, source_target_pairs={{0,2},{4,6},{2,0},{6,4},{1,3},{5,7},{3,1},{7,5},{8,10},{12,14},{10... | collective-permute-start | bytes 393224 | tf_op jit(solution)/shard_map/ppermute | solution.py:358
  13.1 5.3 %collective-permute-start.4 = (f32[1,4,64,128]{3,2,1,0:T(8,128)S(1)}, f32[1,4,64,128]{3,2,1,0:T(8,128)S(1)}, u32[]{:S(2)}, u32[]{:S(2)}) collective-permute-start(f32[1,4,64,128]{3,2,1,0:T(8,128)S(1)} %get-tuple-element.35), channel_id=1, source_target_pairs={{2,4},{6,0},{4,2},{0,6},{3,5},{7,1},{5,3},{1,7},{10,12},{14,8},{12... | collective-permute-start | bytes 393224 | tf_op jit(solution)/shard_map/ppermute | solution.py:358
  18.4 3.3 %collective-permute-start.6 = (f32[2,2,128,128]{3,2,1,0:T(8,128)S(1)}, f32[2,2,128,128]{3,2,1,0:T(8,128)S(1)}, u32[]{:S(2)}, u32[]{:S(2)}) collective-permute-start(f32[2,2,128,128]{3,2,1,0:T(8,128)S(1)} %collective-permute-done.5.refs_0_.refs_7_), channel_id=1, source_target_pairs={{0,2},{4,6},{2,0},{6,4},{1,3},{5,7},{3,1},{7,5},{8,10},{12,14},{10... | collective-permute-start | bytes 786440 | tf_op jit(solution)/shard_map/ppermute | solution.py:360
  21.7 8.6 %copy-start.2 = (f32[1,1,1,128,128]{4,3,2,1,0:T(8,128)S(1)}, f32[1,1,1,128,128]{4,3,2,1,0:T(8,128)}, u32[]{:S(2)}) copy-start(f32[1,1,1,128,128]{4,3,2,1,0:T(8,128)} %param.8) | copy-start | bytes 196612
  23.9 6.4 %collective-permute-start.8 = (f32[128,128]{1,0:T(8,128)S(1)}, f32[128,128]{1,0:T(8,128)S(1)}, u32[]{:S(2)}, u32[]{:S(2)}) collective-permute-start(f32[128,128]{1,0:T(8,128)S(1)} %get-tuple-element.40.refs_2_), channel_id=1, source_target_pairs={{0,8},{16,24},{8,0},{24,16},{1,9},{17,25},{9,1},{25,17},{2,10},{18... | collective-permute-start | bytes 196616 | tf_op jit(solution)/shard_map/ppermute | solution.py:375
  26.7 3.7 %collective-permute-start.7 = (s32[2,8,128]{2,1,0:T(8,128)S(1)}, s32[2,8,128]{2,1,0:T(8,128)S(1)}, u32[]{:S(2)}, u32[]{:S(2)}) collective-permute-start(s32[2,8,128]{2,1,0:T(8,128)S(1)} %get-tuple-element.41.refs_0_.place_ref), channel_id=1, source_target_pairs={{0,1},{1,0},{2,3},{3,2},{4,5},{5,4},{6,7},{7,6},{8,9},{9,8},{10,11... | collective-permute-start | bytes 24584 | tf_op jit(solution)/shard_map/ppermute | solution.py:377
  34.7 6.6 %collective-permute-start.9 = (f32[2,128,128]{2,1,0:T(8,128)S(1)}, f32[2,128,128]{2,1,0:T(8,128)S(1)}, u32[]{:S(2)}, u32[]{:S(2)}) collective-permute-start(f32[2,128,128]{2,1,0:T(8,128)S(1)} %get-tuple-element.47), channel_id=1, source_target_pairs={{0,8},{16,24},{8,0},{24,16},{1,9},{17,25},{9,1},{25,17},{2,10},{18... | collective-permute-start | bytes 393224 | tf_op jit(solution)/shard_map/ppermute | solution.py:386
  35.6 4.8 %collective-permute-start.10 = (f32[128,128]{1,0:T(8,128)S(1)}, f32[128,128]{1,0:T(8,128)S(1)}, u32[]{:S(2)}, u32[]{:S(2)}) collective-permute-start(f32[128,128]{1,0:T(8,128)S(1)} %get-tuple-element.48), channel_id=1, source_target_pairs={{0,1},{1,0},{2,3},{3,2},{4,5},{5,4},{6,7},{7,6},{8,9},{9,8},{10,11... | collective-permute-start | bytes 196616 | tf_op jit(solution)/shard_map/ppermute | solution.py:387
  36.1 5.2 %collective-permute-start.11 = (f32[128,128]{1,0:T(8,128)S(1)}, f32[128,128]{1,0:T(8,128)S(1)}, u32[]{:S(2)}, u32[]{:S(2)}) collective-permute-start(f32[128,128]{1,0:T(8,128)S(1)} %get-tuple-element.49), channel_id=1, source_target_pairs={{0,9},{1,8},{16,25},{17,24},{8,1},{9,0},{24,17},{25,16},{2,11},{3,... | collective-permute-start | bytes 196616 | tf_op jit(solution)/shard_map/ppermute | solution.py:391
  41.7 3.8 %collective-permute-start.12 = (f32[2,64,128]{2,1,0:T(8,128)S(1)}, f32[2,64,128]{2,1,0:T(8,128)S(1)}, u32[]{:S(2)}, u32[]{:S(2)}) collective-permute-start(f32[2,64,128]{2,1,0:T(8,128)S(1)} %get-tuple-element.51), channel_id=1, source_target_pairs={{2,4},{6,0},{4,2},{0,6},{3,5},{7,1},{5,3},{1,7},{10,12},{14,8},{12... | collective-permute-start | bytes 196616 | tf_op jit(solution)/shard_map/ppermute | solution.py:398
  41.7 3.7 %collective-permute-start.13 = (f32[2,64,128]{2,1,0:T(8,128)S(1)}, f32[2,64,128]{2,1,0:T(8,128)S(1)}, u32[]{:S(2)}, u32[]{:S(2)}) collective-permute-start(f32[2,64,128]{2,1,0:T(8,128)S(1)} %get-tuple-element.52), channel_id=1, source_target_pairs={{0,2},{4,6},{2,0},{6,4},{1,3},{5,7},{3,1},{7,5},{8,10},{12,14},{10... | collective-permute-start | bytes 196616 | tf_op jit(solution)/shard_map/ppermute | solution.py:398

commit v2 on v1

--- a/solution.py
+++ b/solution.py
@@ -117,22 +117,26 @@
             real, imag = tile_ref[s, 0], tile_ref[s, 1]
             to_right = jnp.where(lower, half_roll(real), imag)
             to_left = jnp.where(lower, real, half_roll(imag))
-            message_ref[s] = jnp.where(right, to_right, to_left)
+            message_ref[s * det : (s + 1) * det] = jnp.where(right, to_right, to_left)
     for move in others:
         move.wait()
     for dim in range(2):
         place_ref[dim] = jnp.full(place_ref.shape[1:], place_smem[dim], jnp.int32)
+    for message_ref in message_refs:
+        message_ref[slices * det :] = place_ref[0].astype(F32)
 
 
 def corner_kernel(parities, row_axis, *refs):
     count = len(parities)
-    message_refs, corner_refs = refs[:count], refs[count + 2 :]
-    det = message_refs[0].shape[1]
+    message_refs, corner_refs, place_refs = refs[:count], refs[count + 2 : count + 4], refs[count + 4 :]
+    _, slices, half, det = corner_refs[0].shape
     row_parity = lax.rem(lax.axis_index(row_axis), 2)
-    for edge, corner_ref in enumerate(corner_refs):
-        first = half_rows(det, row_parity, edge)
-        for j, message_ref in enumerate(message_refs):
-            corner_ref[j] = message_ref[:, pl.ds(first, det // 2)]
+    for j, (message_ref, place_ref) in enumerate(zip(message_refs, place_refs)):
+        place_ref[...] = message_ref[slices * det :].astype(jnp.int32)
+        for edge, corner_ref in enumerate(corner_refs):
+            first = half_rows(det, row_parity, edge)
+            for s in range(slices):
+                corner_ref[j, s] = message_ref[pl.ds(s * det + first, half)]
 
 
 class Window:
@@ -154,7 +158,7 @@
         det = self.tile.shape[-1]
         lanes = iota((det, det), 1)
         lower, late = lanes < det // 2, lanes >= self.col
-        messages = [self.rows_of(self.corners, (j, s), ref[s]) for j, ref in enumerate(self.messages)]
+        messages = [self.rows_of(self.corners, (j, s), ref[s * det : (s + 1) * det]) for j, ref in enumerate(self.messages)]
         for c in range(2):
             own = half_roll(self.rows_of(self.edges, (s, c), self.tile[s, c]))
             left, right = jnp.zeros_like(own), jnp.zeros_like(own)
@@ -287,7 +291,7 @@
     for parity, partner_ref, one_ref, two_ref in zip(parities, place_refs, one_refs, two_refs):
         strip = jnp.where(has_partner(column_axis, parity), one_ref[...] + two_ref[...], 0.0)
         at_right = is_right(column, parity)
-        for block, part in enumerate(placed(strip, scalar(partner_ref, 0))):
+        for block, part in enumerate(placed(strip, scalar(partner_ref))):
             turned = half_roll(part)
             real = jnp.where(lower != at_right, jnp.where(at_right, turned, part), 0.0)
             imag = jnp.where(lower != at_right, jnp.where(at_right, part, turned), 0.0)
@@ -336,13 +340,13 @@
     place, tile, part, even, odd, *messages = call(
         functools.partial(start_kernel, parities, "ty", "tx"),
         [
-            jax.ShapeDtypeStruct((2, 8, 128), jnp.int32),
+            jax.ShapeDtypeStruct((2, 8, det), jnp.int32),
             shape(*object_slices.shape),
             shape(modes_here // SHARES, 2, det, det),
             shape(slices, 2, half, det),
             shape(slices, 2, half, det),
         ]
-        + [shape(slices, det, det)] * count,
+        + [shape(slices * det + 8, det)] * count,
         [pltpu.with_memory_space_constraint(x, pltpu.HBM) for x in (positions.reshape(2), object_slices, probe_modes)],
         scratch=[pltpu.SMEM((2,), jnp.int32), pltpu.SemaphoreType.DMA((slices + 4,))],
         in_spec=HBM_SPEC,
@@ -350,11 +354,12 @@
     fetched = lax.ppermute(part, "mode", mirror)
     messages = [lax.ppermute(block, "tx", edges(width, parity)) for parity, block in zip(parities, messages)]
     borders = [lax.ppermute(block, "ty", edges(height, edge)) for edge, block in enumerate((even, odd))]
-    corners = call(
+    packed = call(
         functools.partial(corner_kernel, parities, "ty"),
-        [shape(count, slices, half, det)] * 2,
+        [shape(count, slices, half, det)] * 2 + [jax.ShapeDtypeStruct((8, det), jnp.int32)] * count,
         [*messages, *borders],
     )
+    corners, partner_places = packed[:2], packed[2:]
     corners = [lax.ppermute(block, "ty", edges(height, edge)) for edge, block in enumerate(corners)]
     fetched, *_ = lax.optimization_barrier((fetched, *corners))
     fetched = [fetched, lax.ppermute(fetched, "ty", edges(height, 0))]
@@ -373,8 +378,6 @@
         functools.partial(forward_kernel, SHARES), states(modes_here), [window, table, *fetched, mine]
     )
     other = lax.ppermute(mine, "mode", neighbour)
-    place, _ = lax.optimization_barrier((place, mine))
-    partner_places = [lax.ppermute(place, "tx", edges(width, parity)) for parity in parities]
     amplitudes = measured.reshape(det, det)
     center, send, *strips = call(
         functools.partial(backward_kernel, parities, (1, SHARES), "mode", "tx"),

time: 46.3 us -> 46.7 us (level)
  Pallas kernels: 11.4 us -> 11.9 us
  starting transfers between devices: 16.7 us -> 17.2 us
  waiting for transfers between devices: 17.2 us -> 16.7 us
    ppermute x2, waiting for transfers between devices: 3.78 us -> 0.27 us  [body(): lax.ppermute(block, 'tx', edges(width, parity))]
    ppermute x1 -> x0, waiting for transfers between devices: 3.04 us -> none  [body(): lax.ppermute(place, 'tx', edges(width, parity))]
    ppermute x1, waiting for transfers between devices: 0.01 us -> 2.75 us  [body(): other = lax.ppermute(mine, 'mode', neighbour)]
    ppermute x1, waiting for transfers between devices: 0.97 us -> 3.47 us  [body(): twos.append(lax.ppermute(block, ('mode', 'tx'), route))]
    ppermute x2, starting transfers between devices: 2.05 us -> 4.5 us  [body(): lax.ppermute(block, 'tx', edges(width, parity))]
    ppermute x1, starting transfers between devices: 2.1 us -> 0.26 us  [body(): twos.append(lax.ppermute(block, ('mode', 'tx'), route))]
    ppermute x6, waiting for transfers between devices: 6.78 us -> 8.39 us  [body(): lax.ppermute(block, 'ty', edges(height, edge))]
    ppermute x1, starting transfers between devices: 0.89 us -> 1.81 us  [body(): received = lax.ppermute(send, 'mode', neighbour)]
  transfers between devices with their start and end apart: 14 -> 13, of which waited for: 8 -> 7; matrix products, arithmetic and copies ran while one was open for 0% -> 0% of each run, Pallas kernels for 6% -> 6%
where the time goes in v2:
time: 46.7 us; the launch traced here: 46.5 us
  starting transfers between devices  17.2 us (37%)
  waiting for transfers between devices  16.7 us (36%)
  Pallas kernels  11.9 us (25%)
  other arithmetic  0.69 us (1%)
    pallas_call x6, Pallas kernels, call(): pl.pallas_call(kernel, out_shape=outs, in_specs=[in_spec] * len(operands)...  11.9 us
    ppermute x6, waiting for transfers between devices, body(): lax.ppermute(block, 'ty', edges(height, edge))  8.39 us
    ppermute x2, starting transfers between devices, body(): lax.ppermute(block, 'tx', edges(width, parity))  4.5 us
    ppermute x6, starting transfers between devices, body(): lax.ppermute(block, 'ty', edges(height, edge))  4.28 us
    ppermute x1, starting transfers between devices, body(): fetched = lax.ppermute(part, 'mode', mirror)  3.6 us
    ppermute x1, waiting for transfers between devices, body(): twos.append(lax.ppermute(block, ('mode', 'tx'), route))  3.47 us
    ppermute x1, waiting for transfers between devices, body(): other = lax.ppermute(mine, 'mode', neighbour)  2.75 us
    ppermute x1, starting transfers between devices, body(): other = lax.ppermute(mine, 'mode', neighbour)  2.67 us
  transfers between devices with their start and end apart: 13, of which 7 were waited for; matrix products, arithmetic and copies ran while one was open for 0% of the time, Pallas kernels for 6%

profile of v2, /device:TPU:0, one launch (start us, length us, event | category | flops | bytes accessed | tf_op | source)
XLA Modules:
  0.0 46.5 jit_solution(7699872893297160797)
XLA Ops:
  0.0 0.0 copy-start
  0.0 0.0 copy-start.1
  0.0 1.6 %shard_map.55 = (s32[2,8,128]{2,1,0:T(8,128)S(1)}, f32[4,2,128,128]{3,2,1,0:T(8,128)S(1)}, f32[2,2,128,128]{3,2,1,0:T(8,128)S(1)}, f32[4,2,64,128]{3,2,1,0:T(8,1...) custom-call(s32[2]{0:T(128)} %bitcast.5, f32[4,2,128,128]{3,2,1,0:T(8,128)} %tile_hbm.1, ...), custom_call_target="tpu_custom_call" | custom-call | tf_op jit(solution)/shard_map/pallas_call | solution.py:313
  1.6 3.0 %collective-permute-start = (f32[520,128]{1,0:T(8,128)S(1)}, f32[520,128]{1,0:T(8,128)S(1)}, u32[]{:S(2)}, u32[]{:S(2)}) collective-permute-start(f32[520,128]{1,0:T(8,128)S(1)} %get-tuple-element.30), channel_id=1, source_target_pairs={{0,1},{1,0},{2,3},{3,2},{4,5},{5,4},{6,7},{7,6},{8,9},{9,8},{10,11... | collective-permute-start | bytes 798728 | tf_op jit(solution)/shard_map/ppermute | solution.py:355
  4.6 0.0 collective-permute-start.1
  4.6 1.6 %collective-permute-start.2 = (f32[4,2,64,128]{3,2,1,0:T(8,128)S(1)}, f32[4,2,64,128]{3,2,1,0:T(8,128)S(1)}, u32[]{:S(2)}, u32[]{:S(2)}) collective-permute-start(f32[4,2,64,128]{3,2,1,0:T(8,128)S(1)} %get-tuple-element.32), channel_id=1, source_target_pairs={{2,4},{6,0},{4,2},{0,6},{3,5},{7,1},{5,3},{1,7},{10,12},{14,8},{12... | collective-permute-start | bytes 786440 | tf_op jit(solution)/shard_map/ppermute | solution.py:356
  6.2 3.6 %collective-permute-start.5 = (f32[2,2,128,128]{3,2,1,0:T(8,128)S(1)}, f32[2,2,128,128]{3,2,1,0:T(8,128)S(1)}, u32[]{:S(2)}, u32[]{:S(2)}) collective-permute-start(f32[2,2,128,128]{3,2,1,0:T(8,128)S(1)} %get-tuple-element.38), channel_id=1, source_target_pairs={{0,24},{8,16},{16,8},{24,0},{1,25},{9,17},{17,9},{25,1},{2,26},{10... | collective-permute-start | bytes 786440 | tf_op jit(solution)/shard_map/ppermute | solution.py:354
  9.8 0.0 collective-permute-done.1.refs_1_.refs_2_
  9.8 2.7 %collective-permute-done.2.refs_2_.refs_3_ = f32[4,2,64,128]{3,2,1,0:T(8,128)S(1)} collective-permute-done((f32[4,2,64,128]{3,2,1,0:T(8,128)S(1)}, f32[4,2,64,128]{3,2,1,0:T(8,128)S(1)}, u32[]{:S(2)}, u32[]{:S(2)}) %collective-permute-start.2) | collective-permute-done | bytes 262176 | tf_op jit(solution)/shard_map/ppermute | solution.py:356
  12.5 0.0 collective-permute-done.refs_0_.refs_6_
  12.6 0.8 %collective-permute-start.3 = (f32[1,4,64,128]{3,2,1,0:T(8,128)S(1)}, f32[1,4,64,128]{3,2,1,0:T(8,128)S(1)}, u32[]{:S(2)}, u32[]{:S(2)}) collective-permute-start(f32[1,4,64,128]{3,2,1,0:T(8,128)S(1)} %get-tuple-element.35), channel_id=1, source_target_pairs={{0,2},{4,6},{2,0},{6,4},{1,3},{5,7},{3,1},{7,5},{8,10},{12,14},{10... | collective-permute-start | bytes 393224 | tf_op jit(solution)/shard_map/ppermute | solution.py:363
  13.4 1.2 %collective-permute-start.4 = (f32[1,4,64,128]{3,2,1,0:T(8,128)S(1)}, f32[1,4,64,128]{3,2,1,0:T(8,128)S(1)}, u32[]{:S(2)}, u32[]{:S(2)}) collective-permute-start(f32[1,4,64,128]{3,2,1,0:T(8,128)S(1)} %get-tuple-element.36), channel_id=1, source_target_pairs={{2,4},{6,0},{4,2},{0,6},{3,5},{7,1},{5,3},{1,7},{10,12},{14,8},{12... | collective-permute-start | bytes 393224 | tf_op jit(solution)/shard_map/ppermute | solution.py:363
  14.6 1.8 %collective-permute-done.5.refs_0_.refs_7_ = f32[2,2,128,128]{3,2,1,0:T(8,128)S(1)} collective-permute-done((f32[2,2,128,128]{3,2,1,0:T(8,128)S(1)}, f32[2,2,128,128]{3,2,1,0:T(8,128)S(1)}, u32[]{:S(2)}, u32[]{:S(2)}) %collective-permute-start.5) | collective-permute-done | bytes 262176 | tf_op jit(solution)/shard_map/ppermute | solution.py:354
  16.4 0.0 collective-permute-done.3.refs_4_
  16.4 2.5 %collective-permute-done.4.refs_5_ = f32[1,4,64,128]{3,2,1,0:T(8,128)S(1)} collective-permute-done((f32[1,4,64,128]{3,2,1,0:T(8,128)S(1)}, f32[1,4,64,128]{3,2,1,0:T(8,128)S(1)}, u32[]{:S(2)}, u32[]{:S(2)}) %collective-permute-start.4) | collective-permute-done | bytes 131104 | tf_op jit(solution)/shard_map/ppermute | solution.py:363
  18.9 0.1 collective-permute-start.6
  19.0 0.0 copy-done
  19.0 0.0 copy-done.1
  19.1 2.9 %shard_map.57 = (f32[4,2,128,128]{3,2,1,0:T(8,128)S(1)}, f32[3,4,2,128,128]{4,3,2,1,0:T(8,128)S(1)}, f32[4,2,128,128]{3,2,1,0:T(8,128)S(1)}, f32[128,128]{1,0:T(8,128)S(1)}) custom-call(bf16[8,256,256]{2,1,0:T(8,128)(2,1)S(1)} %copy-done, f32[4,2,128,128]{3,2,1,0:T(8,128)S(1)} %copy-done.1, s32[2,8,128]{2,1,0:T(8,128)S(1)} %get-tuple-element.29.refs_0_.place_ref, ...), custom_call_target="tpu_custom_call" | custom-call | tf_op jit(solution)/shard_map/pallas_call | solution.py:313
  22.0 0.0 copy-start.2
  22.0 0.0 collective-permute-done.6.refs_1_.refs_8_
  22.0 2.3 %shard_map.58 = (f32[3,4,2,128,128]{4,3,2,1,0:T(8,128)S(1)}, f32[4,2,128,128]{3,2,1,0:T(8,128)S(1)}, f32[128,128]{1,0:T(8,128)S(1)}) custom-call(f32[4,2,128,128]{3,2,1,0:T(8,128)S(1)} %get-tuple-element.37.window_ref.refs_5_, bf16[8,256,256]{2,1,0:T(8,128)(2,1)S(1)} %copy-done, f32[2,2,128,128]{3,2,1,0:T(8,128)S(1)} %collective-permute-done.5.refs_0_.refs_7_, ...), custom_call_target="tpu_custom_call" | custom-call | tf_op jit(solution)/shard_map/pallas_call | solution.py:313
  24.3 2.7 %collective-permute-start.7 = (f32[128,128]{1,0:T(8,128)S(1)}, f32[128,128]{1,0:T(8,128)S(1)}, u32[]{:S(2)}, u32[]{:S(2)}) collective-permute-start(f32[128,128]{1,0:T(8,128)S(1)} %get-tuple-element.41.refs_2_), channel_id=1, source_target_pairs={{0,8},{16,24},{8,0},{24,16},{1,9},{17,25},{9,1},{25,17},{2,10},{18... | collective-permute-start | bytes 196616 | tf_op jit(solution)/shard_map/ppermute | solution.py:380
  26.9 2.7 %collective-permute-done.7.refs_3_ = f32[128,128]{1,0:T(8,128)S(1)} collective-permute-done((f32[128,128]{1,0:T(8,128)S(1)}, f32[128,128]{1,0:T(8,128)S(1)}, u32[]{:S(2)}, u32[]{:S(2)}) %collective-permute-start.7) | collective-permute-done | bytes 65568 | tf_op jit(solution)/shard_map/ppermute | solution.py:380
  29.7 0.0 copy-done.2
  29.7 4.7 %shard_map.59 = (f32[2,128,128]{2,1,0:T(8,128)S(1)}, f32[2,128,128]{2,1,0:T(8,128)S(1)}, f32[128,128]{1,0:T(8,128)S(1)}, f32[128,128]{1,0:T(8,128)S(1)}) custom-call(s32[2,8,128]{2,1,0:T(8,128)S(1)} %get-tuple-element.29.refs_0_.place_ref, s32[8,128]{1,0:T(8,128)S(1)} %get-tuple-element.33.refs_0_, f32[128,128]{1,0:T(8,128)S(1)} %bitcast.4, ...), custom_call_target="tpu_custom_call" | custom-call | tf_op jit(solution)/shard_map/pallas_call | solution.py:313
  34.4 1.8 %collective-permute-start.8 = (f32[2,128,128]{2,1,0:T(8,128)S(1)}, f32[2,128,128]{2,1,0:T(8,128)S(1)}, u32[]{:S(2)}, u32[]{:S(2)}) collective-permute-start(f32[2,128,128]{2,1,0:T(8,128)S(1)} %get-tuple-element.47), channel_id=1, source_target_pairs={{0,8},{16,24},{8,0},{24,16},{1,9},{17,25},{9,1},{25,17},{2,10},{18... | collective-permute-start | bytes 393224 | tf_op jit(solution)/shard_map/ppermute | solution.py:389
  36.2 0.3 collective-permute-start.10
  36.5 1.5 %collective-permute-start.9 = (f32[128,128]{1,0:T(8,128)S(1)}, f32[128,128]{1,0:T(8,128)S(1)}, u32[]{:S(2)}, u32[]{:S(2)}) collective-permute-start(f32[128,128]{1,0:T(8,128)S(1)} %get-tuple-element.48), channel_id=1, source_target_pairs={{0,1},{1,0},{2,3},{3,2},{4,5},{5,4},{6,7},{7,6},{8,9},{9,8},{10,11... | collective-permute-start | bytes 196616 | tf_op jit(solution)/shard_map/ppermute | solution.py:390
  38.0 3.5 %collective-permute-done.10.refs_2_ = f32[128,128]{1,0:T(8,128)S(1)} collective-permute-done((f32[128,128]{1,0:T(8,128)S(1)}, f32[128,128]{1,0:T(8,128)S(1)}, u32[]{:S(2)}, u32[]{:S(2)}) %collective-permute-start.10) | collective-permute-done | bytes 65568 | tf_op jit(solution)/shard_map/ppermute | solution.py:394
  41.5 0.3 collective-permute-done.9.refs_1_
  41.7 0.0 collective-permute-done.8.other_ref
  41.7 0.3 shard_map.60
  42.1 0.1 collective-permute-start.11
  42.2 0.5 %collective-permute-start.12 = (f32[2,64,128]{2,1,0:T(8,128)S(1)}, f32[2,64,128]{2,1,0:T(8,128)S(1)}, u32[]{:S(2)}, u32[]{:S(2)}) collective-permute-start(f32[2,64,128]{2,1,0:T(8,128)S(1)} %get-tuple-element.52), channel_id=1, source_target_pairs={{0,2},{4,6},{2,0},{6,4},{1,3},{5,7},{3,1},{7,5},{8,10},{12,14},{10... | collective-permute-start | bytes 196616 | tf_op jit(solution)/shard_map/ppermute | solution.py:401
  42.7 3.1 %collective-permute-done.11 = f32[2,64,128]{2,1,0:T(8,128)S(1)} collective-permute-done((f32[2,64,128]{2,1,0:T(8,128)S(1)}, f32[2,64,128]{2,1,0:T(8,128)S(1)}, u32[]{:S(2)}, u32[]{:S(2)}) %collective-permute-start.11) | collective-permute-done | bytes 65568 | tf_op jit(solution)/shard_map/ppermute | solution.py:401
  45.8 0.0 collective-permute-done.12
  45.9 0.7 %fusion = f32[1,2,128,128]{3,2,1,0:T(8,128)} fusion(f32[2,128,128]{2,1,0:T(8,128)S(1)} %get-tuple-element.50, f32[2,64,128]{2,1,0:T(8,128)S(1)} %get-tuple-element.54, f32[2,64,128]{2,1,0:T(8,128)S(1)} %get-tuple-element.53), kind=kLoop, calls=%fused_computation.1 | loop fusion | flops 65536 | bytes 393216 | tf_op jit(solution)/shard_map/broadcast_in_dim | solution.py:406
  (2 shorter events, 0.0 us)
Async XLA Ops:
  0.0 19.0 %copy-start = (bf16[8,256,256]{2,1,0:T(8,128)(2,1)S(1)}, bf16[8,256,256]{2,1,0:T(8,128)(2,1)}, u32[]{:S(2)}) copy-start(bf16[8,256,256]{2,1,0:T(8,128)(2,1)} %constant.21.clone.table_ref.refs_4_) | copy-start | bytes 3145732
  0.0 19.0 %copy-start.1 = (f32[4,2,128,128]{3,2,1,0:T(8,128)S(1)}, f32[4,2,128,128]{3,2,1,0:T(8,128)}, u32[]{:S(2)}) copy-start(f32[4,2,128,128]{3,2,1,0:T(8,128)} %refs_6_.1) | copy-start | bytes 1572868
  1.6 11.0 %collective-permute-start = (f32[520,128]{1,0:T(8,128)S(1)}, f32[520,128]{1,0:T(8,128)S(1)}, u32[]{:S(2)}, u32[]{:S(2)}) collective-permute-start(f32[520,128]{1,0:T(8,128)S(1)} %get-tuple-element.30), channel_id=1, source_target_pairs={{0,1},{1,0},{2,3},{3,2},{4,5},{5,4},{6,7},{7,6},{8,9},{9,8},{10,11... | collective-permute-start | bytes 798728 | tf_op jit(solution)/shard_map/ppermute | solution.py:355
  4.6 5.2 %collective-permute-start.1 = (f32[4,2,64,128]{3,2,1,0:T(8,128)S(1)}, f32[4,2,64,128]{3,2,1,0:T(8,128)S(1)}, u32[]{:S(2)}, u32[]{:S(2)}) collective-permute-start(f32[4,2,64,128]{3,2,1,0:T(8,128)S(1)} %get-tuple-element.31), channel_id=1, source_target_pairs={{0,2},{4,6},{2,0},{6,4},{1,3},{5,7},{3,1},{7,5},{8,10},{12,14},{10... | collective-permute-start | bytes 786440 | tf_op jit(solution)/shard_map/ppermute | solution.py:356
  4.6 8.0 %collective-permute-start.2 = (f32[4,2,64,128]{3,2,1,0:T(8,128)S(1)}, f32[4,2,64,128]{3,2,1,0:T(8,128)S(1)}, u32[]{:S(2)}, u32[]{:S(2)}) collective-permute-start(f32[4,2,64,128]{3,2,1,0:T(8,128)S(1)} %get-tuple-element.32), channel_id=1, source_target_pairs={{2,4},{6,0},{4,2},{0,6},{3,5},{7,1},{5,3},{1,7},{10,12},{14,8},{12... | collective-permute-start | bytes 786440 | tf_op jit(solution)/shard_map/ppermute | solution.py:356
  6.2 10.2 %collective-permute-start.5 = (f32[2,2,128,128]{3,2,1,0:T(8,128)S(1)}, f32[2,2,128,128]{3,2,1,0:T(8,128)S(1)}, u32[]{:S(2)}, u32[]{:S(2)}) collective-permute-start(f32[2,2,128,128]{3,2,1,0:T(8,128)S(1)} %get-tuple-element.38), channel_id=1, source_target_pairs={{0,24},{8,16},{16,8},{24,0},{1,25},{9,17},{17,9},{25,1},{2,26},{10... | collective-permute-start | bytes 786440 | tf_op jit(solution)/shard_map/ppermute | solution.py:354
  12.6 3.8 %collective-permute-start.3 = (f32[1,4,64,128]{3,2,1,0:T(8,128)S(1)}, f32[1,4,64,128]{3,2,1,0:T(8,128)S(1)}, u32[]{:S(2)}, u32[]{:S(2)}) collective-permute-start(f32[1,4,64,128]{3,2,1,0:T(8,128)S(1)} %get-tuple-element.35), channel_id=1, source_target_pairs={{0,2},{4,6},{2,0},{6,4},{1,3},{5,7},{3,1},{7,5},{8,10},{12,14},{10... | collective-permute-start | bytes 393224 | tf_op jit(solution)/shard_map/ppermute | solution.py:363
  13.4 5.5 %collective-permute-start.4 = (f32[1,4,64,128]{3,2,1,0:T(8,128)S(1)}, f32[1,4,64,128]{3,2,1,0:T(8,128)S(1)}, u32[]{:S(2)}, u32[]{:S(2)}) collective-permute-start(f32[1,4,64,128]{3,2,1,0:T(8,128)S(1)} %get-tuple-element.36), channel_id=1, source_target_pairs={{2,4},{6,0},{4,2},{0,6},{3,5},{7,1},{5,3},{1,7},{10,12},{14,8},{12... | collective-permute-start | bytes 393224 | tf_op jit(solution)/shard_map/ppermute | solution.py:363
  18.9 3.1 %collective-permute-start.6 = (f32[2,2,128,128]{3,2,1,0:T(8,128)S(1)}, f32[2,2,128,128]{3,2,1,0:T(8,128)S(1)}, u32[]{:S(2)}, u32[]{:S(2)}) collective-permute-start(f32[2,2,128,128]{3,2,1,0:T(8,128)S(1)} %collective-permute-done.5.refs_0_.refs_7_), channel_id=1, source_target_pairs={{0,2},{4,6},{2,0},{6,4},{1,3},{5,7},{3,1},{7,5},{8,10},{12,14},{10... | collective-permute-start | bytes 786440 | tf_op jit(solution)/shard_map/ppermute | solution.py:365
  22.0 7.7 %copy-start.2 = (f32[1,1,1,128,128]{4,3,2,1,0:T(8,128)S(1)}, f32[1,1,1,128,128]{4,3,2,1,0:T(8,128)}, u32[]{:S(2)}) copy-start(f32[1,1,1,128,128]{4,3,2,1,0:T(8,128)} %param.8) | copy-start | bytes 196612
  24.3 5.4 %collective-permute-start.7 = (f32[128,128]{1,0:T(8,128)S(1)}, f32[128,128]{1,0:T(8,128)S(1)}, u32[]{:S(2)}, u32[]{:S(2)}) collective-permute-start(f32[128,128]{1,0:T(8,128)S(1)} %get-tuple-element.41.refs_2_), channel_id=1, source_target_pairs={{0,8},{16,24},{8,0},{24,16},{1,9},{17,25},{9,1},{25,17},{2,10},{18... | collective-permute-start | bytes 196616 | tf_op jit(solution)/shard_map/ppermute | solution.py:380
  34.4 7.3 %collective-permute-start.8 = (f32[2,128,128]{2,1,0:T(8,128)S(1)}, f32[2,128,128]{2,1,0:T(8,128)S(1)}, u32[]{:S(2)}, u32[]{:S(2)}) collective-permute-start(f32[2,128,128]{2,1,0:T(8,128)S(1)} %get-tuple-element.47), channel_id=1, source_target_pairs={{0,8},{16,24},{8,0},{24,16},{1,9},{17,25},{9,1},{25,17},{2,10},{18... | collective-permute-start | bytes 393224 | tf_op jit(solution)/shard_map/ppermute | solution.py:389
  36.2 5.2 %collective-permute-start.10 = (f32[128,128]{1,0:T(8,128)S(1)}, f32[128,128]{1,0:T(8,128)S(1)}, u32[]{:S(2)}, u32[]{:S(2)}) collective-permute-start(f32[128,128]{1,0:T(8,128)S(1)} %get-tuple-element.49), channel_id=1, source_target_pairs={{0,9},{1,8},{16,25},{17,24},{8,1},{9,0},{24,17},{25,16},{2,11},{3,... | collective-permute-start | bytes 196616 | tf_op jit(solution)/shard_map/ppermute | solution.py:394
  36.5 5.2 %collective-permute-start.9 = (f32[128,128]{1,0:T(8,128)S(1)}, f32[128,128]{1,0:T(8,128)S(1)}, u32[]{:S(2)}, u32[]{:S(2)}) collective-permute-start(f32[128,128]{1,0:T(8,128)S(1)} %get-tuple-element.48), channel_id=1, source_target_pairs={{0,1},{1,0},{2,3},{3,2},{4,5},{5,4},{6,7},{7,6},{8,9},{9,8},{10,11... | collective-permute-start | bytes 196616 | tf_op jit(solution)/shard_map/ppermute | solution.py:390
  42.1 3.8 %collective-permute-start.11 = (f32[2,64,128]{2,1,0:T(8,128)S(1)}, f32[2,64,128]{2,1,0:T(8,128)S(1)}, u32[]{:S(2)}, u32[]{:S(2)}) collective-permute-start(f32[2,64,128]{2,1,0:T(8,128)S(1)} %get-tuple-element.51), channel_id=1, source_target_pairs={{2,4},{6,0},{4,2},{0,6},{3,5},{7,1},{5,3},{1,7},{10,12},{14,8},{12... | collective-permute-start | bytes 196616 | tf_op jit(solution)/shard_map/ppermute | solution.py:401
  42.2 3.7 %collective-permute-start.12 = (f32[2,64,128]{2,1,0:T(8,128)S(1)}, f32[2,64,128]{2,1,0:T(8,128)S(1)}, u32[]{:S(2)}, u32[]{:S(2)}) collective-permute-start(f32[2,64,128]{2,1,0:T(8,128)S(1)} %get-tuple-element.52), channel_id=1, source_target_pairs={{0,2},{4,6},{2,0},{6,4},{1,3},{5,7},{3,1},{7,5},{8,10},{12,14},{10... | collective-permute-start | bytes 196616 | tf_op jit(solution)/shard_map/ppermute | solution.py:401

commit v3 on v1

--- a/solution.py
+++ b/solution.py
@@ -11,7 +11,6 @@
 FRESNEL_RATE = 0.3
 F32, BF16 = jnp.float32, jnp.bfloat16
 VMEM_LIMIT = 24 * 2**20
-ROWS = 32
 SHARES = 2
 MOVE, MOVE_BACK, FOURIER, FOURIER_BACK = 0, 2, 4, 6
 
@@ -45,8 +44,9 @@
 
 def one_side(real, imag, table_ref, base):
     high, low = split(jnp.concatenate([real, imag], 1))
-    both = dot(high, table_ref[base]) + dot(low, table_ref[base]) + dot(high, table_ref[base + 1])
-    det = real.shape[1]
+    rows, det = real.shape
+    stacked = dot(jnp.concatenate([high, low], 0), table_ref[base])
+    both = stacked[:rows] + stacked[rows:] + dot(high, table_ref[base + 1])
     return both[:, :det], both[:, det:]
 
 
@@ -236,17 +236,11 @@
             back_real, back_imag = two_sided(pulled_real, pulled_imag, table_ref, base)
             back_ref[now, mode, 0] = back_real
             back_ref[now, mode, 1] = back_imag
-        for first in range(0, det, ROWS):
-            rows = slice(first, first + ROWS)
-            term_real, term_imag = jnp.zeros((ROWS, det), F32), jnp.zeros((ROWS, det), F32)
-            for mode, (k, j) in enumerate(slots):
-                wave = wave_refs[k].at[s - 1, j] if s > 0 else probes[mode]
-                wave_real, wave_imag = wave[0, rows], wave[1, rows]
-                back_real, back_imag = back_ref[now, mode, 0, rows], back_ref[now, mode, 1, rows]
-                term_real = term_real + (wave_real * back_real + wave_imag * back_imag)
-                term_imag = term_imag + (wave_real * back_imag - wave_imag * back_real)
-            term_ref[s, 0, rows] = term_real
-            term_ref[s, 1, rows] = term_imag
+            wave = wave_refs[k].at[s - 1, j] if s > 0 else probes[mode]
+            term_real = wave[0] * back_real + wave[1] * back_imag
+            term_imag = wave[0] * back_imag - wave[1] * back_real
+            term_ref[s, 0] = term_real if mode == 0 else term_ref[s, 0] + term_real
+            term_ref[s, 1] = term_imag if mode == 0 else term_ref[s, 1] + term_imag
         if s % 2 == 1:
             for c in range(2):
                 term_ref[s, c] = term_ref[s, c].T

time: 46.3 us -> 46.1 us (level)
  no operation moved by 1% of the time
where the time goes in v3:
time: 46.1 us; the launch traced here: 45.9 us
  waiting for transfers between devices  17.2 us (37%)
  starting transfers between devices  16.7 us (36%)
  Pallas kernels  11.2 us (24%)
  other arithmetic  0.69 us (1%)
    pallas_call x6, Pallas kernels, call(): pl.pallas_call(kernel, out_shape=outs, in_specs=[in_spec] * len(operands)...  11.2 us
    ppermute x6, waiting for transfers between devices, body(): lax.ppermute(block, 'ty', edges(height, edge))  6.77 us
    ppermute x6, starting transfers between devices, body(): lax.ppermute(block, 'ty', edges(height, edge))  4.35 us
    ppermute x2, waiting for transfers between devices, body(): lax.ppermute(block, 'tx', edges(width, parity))  3.78 us
    ppermute x1, starting transfers between devices, body(): fetched = lax.ppermute(part, 'mode', mirror)  3.6 us
    ppermute x1, waiting for transfers between devices, body(): lax.ppermute(place, 'tx', edges(width, parity))  3.04 us
    ppermute x1, starting transfers between devices, body(): other = lax.ppermute(mine, 'mode', neighbour)  2.73 us
    ppermute x1, waiting for transfers between devices, body(): fetched = lax.ppermute(part, 'mode', mirror)  2.64 us
  transfers between devices with their start and end apart: 14, of which 8 were waited for; matrix products, arithmetic and copies ran while one was open for 0% of the time, Pallas kernels for 6%

profile of v3, /device:TPU:0, one launch (start us, length us, event | category | flops | bytes accessed | tf_op | source)
XLA Modules:
  0.0 45.9 jit_solution(12576214707180840381)
XLA Ops:
  0.0 0.0 copy-start
  0.0 0.0 copy-start.1
  0.0 1.6 %shard_map.55 = (s32[2,8,128]{2,1,0:T(8,128)S(1)}, f32[4,2,128,128]{3,2,1,0:T(8,128)S(1)}, f32[2,2,128,128]{3,2,1,0:T(8,128)S(1)}, f32[4,2,64,128]{3,2,1,0:T(8,1...) custom-call(s32[2]{0:T(128)} %bitcast.5, f32[4,2,128,128]{3,2,1,0:T(8,128)} %tile_hbm.1, ...), custom_call_target="tpu_custom_call" | custom-call | tf_op jit(solution)/shard_map/pallas_call | solution.py:303
  1.6 0.5 %collective-permute-start = (f32[4,2,64,128]{3,2,1,0:T(8,128)S(1)}, f32[4,2,64,128]{3,2,1,0:T(8,128)S(1)}, u32[]{:S(2)}, u32[]{:S(2)}) collective-permute-start(f32[4,2,64,128]{3,2,1,0:T(8,128)S(1)} %get-tuple-element.31), channel_id=1, source_target_pairs={{0,2},{4,6},{2,0},{6,4},{1,3},{5,7},{3,1},{7,5},{8,10},{12,14},{10... | collective-permute-start | bytes 786440 | tf_op jit(solution)/shard_map/ppermute | solution.py:346
  2.1 2.6 %collective-permute-start.1 = (f32[4,2,64,128]{3,2,1,0:T(8,128)S(1)}, f32[4,2,64,128]{3,2,1,0:T(8,128)S(1)}, u32[]{:S(2)}, u32[]{:S(2)}) collective-permute-start(f32[4,2,64,128]{3,2,1,0:T(8,128)S(1)} %get-tuple-element.32), channel_id=1, source_target_pairs={{2,4},{6,0},{4,2},{0,6},{3,5},{7,1},{5,3},{1,7},{10,12},{14,8},{12... | collective-permute-start | bytes 786440 | tf_op jit(solution)/shard_map/ppermute | solution.py:346
  4.7 1.5 %collective-permute-start.2 = (f32[4,128,128]{2,1,0:T(8,128)S(1)}, f32[4,128,128]{2,1,0:T(8,128)S(1)}, u32[]{:S(2)}, u32[]{:S(2)}) collective-permute-start(f32[4,128,128]{2,1,0:T(8,128)S(1)} %get-tuple-element.33), channel_id=1, source_target_pairs={{0,1},{1,0},{2,3},{3,2},{4,5},{5,4},{6,7},{7,6},{8,9},{9,8},{10,11... | collective-permute-start | bytes 786440 | tf_op jit(solution)/shard_map/ppermute | solution.py:345
  6.2 3.6 %collective-permute-start.5 = (f32[2,2,128,128]{3,2,1,0:T(8,128)S(1)}, f32[2,2,128,128]{3,2,1,0:T(8,128)S(1)}, u32[]{:S(2)}, u32[]{:S(2)}) collective-permute-start(f32[2,2,128,128]{3,2,1,0:T(8,128)S(1)} %get-tuple-element.37), channel_id=1, source_target_pairs={{0,24},{8,16},{16,8},{24,0},{1,25},{9,17},{17,9},{25,1},{2,26},{10... | collective-permute-start | bytes 786440 | tf_op jit(solution)/shard_map/ppermute | solution.py:344
  9.8 0.0 collective-permute-done.refs_1_.refs_2_
  9.8 1.5 %collective-permute-done.1.refs_2_.refs_3_ = f32[4,2,64,128]{3,2,1,0:T(8,128)S(1)} collective-permute-done((f32[4,2,64,128]{3,2,1,0:T(8,128)S(1)}, f32[4,2,64,128]{3,2,1,0:T(8,128)S(1)}, u32[]{:S(2)}, u32[]{:S(2)}) %collective-permute-start.1) | collective-permute-done | bytes 262176 | tf_op jit(solution)/shard_map/ppermute | solution.py:346
  11.3 1.7 %collective-permute-done.2.refs_0_.refs_6_ = f32[4,128,128]{2,1,0:T(8,128)S(1)} collective-permute-done((f32[4,128,128]{2,1,0:T(8,128)S(1)}, f32[4,128,128]{2,1,0:T(8,128)S(1)}, u32[]{:S(2)}, u32[]{:S(2)}) %collective-permute-start.2) | collective-permute-done | bytes 262176 | tf_op jit(solution)/shard_map/ppermute | solution.py:345
  13.0 0.1 collective-permute-start.3
  13.1 0.4 collective-permute-start.4
  13.5 2.6 %collective-permute-done.5.refs_0_.refs_7_ = f32[2,2,128,128]{3,2,1,0:T(8,128)S(1)} collective-permute-done((f32[2,2,128,128]{3,2,1,0:T(8,128)S(1)}, f32[2,2,128,128]{3,2,1,0:T(8,128)S(1)}, u32[]{:S(2)}, u32[]{:S(2)}) %collective-permute-start.5) | collective-permute-done | bytes 262176 | tf_op jit(solution)/shard_map/ppermute | solution.py:344
  16.2 0.0 collective-permute-done.3.refs_4_
  16.2 2.2 %collective-permute-done.4.refs_5_ = f32[1,4,64,128]{3,2,1,0:T(8,128)S(1)} collective-permute-done((f32[1,4,64,128]{3,2,1,0:T(8,128)S(1)}, f32[1,4,64,128]{3,2,1,0:T(8,128)S(1)}, u32[]{:S(2)}, u32[]{:S(2)}) %collective-permute-start.4) | collective-permute-done | bytes 131104 | tf_op jit(solution)/shard_map/ppermute | solution.py:352
  18.4 0.4 collective-permute-start.6
  18.8 0.0 copy-done
  18.8 0.0 copy-done.1
  18.8 2.8 %shard_map.57 = (f32[4,2,128,128]{3,2,1,0:T(8,128)S(1)}, f32[3,4,2,128,128]{4,3,2,1,0:T(8,128)S(1)}, f32[4,2,128,128]{3,2,1,0:T(8,128)S(1)}, f32[128,128]{1,0:T(8,128)S(1)}) custom-call(bf16[8,256,256]{2,1,0:T(8,128)(2,1)S(1)} %copy-done, f32[4,2,128,128]{3,2,1,0:T(8,128)S(1)} %copy-done.1, s32[2,8,128]{2,1,0:T(8,128)S(1)} %get-tuple-element.41.refs_0_.place_ref, ...), custom_call_target="tpu_custom_call" | custom-call | tf_op jit(solution)/shard_map/pallas_call | solution.py:303
  21.6 0.0 copy-start.2
  21.6 0.0 collective-permute-done.6.refs_1_.refs_8_
  21.6 2.2 %shard_map.58 = (f32[3,4,2,128,128]{4,3,2,1,0:T(8,128)S(1)}, f32[4,2,128,128]{3,2,1,0:T(8,128)S(1)}, f32[128,128]{1,0:T(8,128)S(1)}) custom-call(f32[4,2,128,128]{3,2,1,0:T(8,128)S(1)} %get-tuple-element.36.window_ref.refs_5_, bf16[8,256,256]{2,1,0:T(8,128)(2,1)S(1)} %copy-done, f32[2,2,128,128]{3,2,1,0:T(8,128)S(1)} %collective-permute-done.5.refs_0_.refs_7_, ...), custom_call_target="tpu_custom_call" | custom-call | tf_op jit(solution)/shard_map/pallas_call | solution.py:303
  23.8 2.7 %collective-permute-start.8 = (f32[128,128]{1,0:T(8,128)S(1)}, f32[128,128]{1,0:T(8,128)S(1)}, u32[]{:S(2)}, u32[]{:S(2)}) collective-permute-start(f32[128,128]{1,0:T(8,128)S(1)} %get-tuple-element.40.refs_2_), channel_id=1, source_target_pairs={{0,8},{16,24},{8,0},{24,16},{1,9},{17,25},{9,1},{25,17},{2,10},{18... | collective-permute-start | bytes 196616 | tf_op jit(solution)/shard_map/ppermute | solution.py:369
  26.6 0.6 %collective-permute-start.7 = (s32[2,8,128]{2,1,0:T(8,128)S(1)}, s32[2,8,128]{2,1,0:T(8,128)S(1)}, u32[]{:S(2)}, u32[]{:S(2)}) collective-permute-start(s32[2,8,128]{2,1,0:T(8,128)S(1)} %get-tuple-element.41.refs_0_.place_ref), channel_id=1, source_target_pairs={{0,1},{1,0},{2,3},{3,2},{4,5},{5,4},{6,7},{7,6},{8,9},{9,8},{10,11... | collective-permute-start | bytes 24584 | tf_op jit(solution)/shard_map/ppermute | solution.py:371
  27.2 3.0 %collective-permute-done.7.refs_0_ = s32[2,8,128]{2,1,0:T(8,128)S(1)} collective-permute-done((s32[2,8,128]{2,1,0:T(8,128)S(1)}, s32[2,8,128]{2,1,0:T(8,128)S(1)}, u32[]{:S(2)}, u32[]{:S(2)}) %collective-permute-start.7) | collective-permute-done | bytes 8224 | tf_op jit(solution)/shard_map/ppermute | solution.py:371
  30.2 0.0 collective-permute-done.8.refs_3_
  30.2 0.0 copy-done.2
  30.2 4.3 %shard_map.59 = (f32[2,128,128]{2,1,0:T(8,128)S(1)}, f32[2,128,128]{2,1,0:T(8,128)S(1)}, f32[128,128]{1,0:T(8,128)S(1)}, f32[128,128]{1,0:T(8,128)S(1)}) custom-call(s32[2,8,128]{2,1,0:T(8,128)S(1)} %get-tuple-element.41.refs_0_.place_ref, s32[2,8,128]{2,1,0:T(8,128)S(1)} %collective-permute-done.7.refs_0_, f32[128,128]{1,0:T(8,128)S(1)} %bitcast.4, ...), custom_call_target="tpu_custom_call" | custom-call | tf_op jit(solution)/shard_map/pallas_call | solution.py:303
  34.5 0.9 %collective-permute-start.9 = (f32[2,128,128]{2,1,0:T(8,128)S(1)}, f32[2,128,128]{2,1,0:T(8,128)S(1)}, u32[]{:S(2)}, u32[]{:S(2)}) collective-permute-start(f32[2,128,128]{2,1,0:T(8,128)S(1)} %get-tuple-element.47), channel_id=1, source_target_pairs={{0,8},{16,24},{8,0},{24,16},{1,9},{17,25},{9,1},{25,17},{2,10},{18... | collective-permute-start | bytes 393224 | tf_op jit(solution)/shard_map/ppermute | solution.py:380
  35.4 0.5 %collective-permute-start.10 = (f32[128,128]{1,0:T(8,128)S(1)}, f32[128,128]{1,0:T(8,128)S(1)}, u32[]{:S(2)}, u32[]{:S(2)}) collective-permute-start(f32[128,128]{1,0:T(8,128)S(1)} %get-tuple-element.48), channel_id=1, source_target_pairs={{0,1},{1,0},{2,3},{3,2},{4,5},{5,4},{6,7},{7,6},{8,9},{9,8},{10,11... | collective-permute-start | bytes 196616 | tf_op jit(solution)/shard_map/ppermute | solution.py:381
  35.9 2.1 %collective-permute-start.11 = (f32[128,128]{1,0:T(8,128)S(1)}, f32[128,128]{1,0:T(8,128)S(1)}, u32[]{:S(2)}, u32[]{:S(2)}) collective-permute-start(f32[128,128]{1,0:T(8,128)S(1)} %get-tuple-element.49), channel_id=1, source_target_pairs={{0,9},{1,8},{16,25},{17,24},{8,1},{9,0},{24,17},{25,16},{2,11},{3,... | collective-permute-start | bytes 196616 | tf_op jit(solution)/shard_map/ppermute | solution.py:385
  38.0 2.1 %collective-permute-done.10.refs_1_ = f32[128,128]{1,0:T(8,128)S(1)} collective-permute-done((f32[128,128]{1,0:T(8,128)S(1)}, f32[128,128]{1,0:T(8,128)S(1)}, u32[]{:S(2)}, u32[]{:S(2)}) %collective-permute-start.10) | collective-permute-done | bytes 65568 | tf_op jit(solution)/shard_map/ppermute | solution.py:381
  40.1 1.0 %collective-permute-done.11.refs_2_ = f32[128,128]{1,0:T(8,128)S(1)} collective-permute-done((f32[128,128]{1,0:T(8,128)S(1)}, f32[128,128]{1,0:T(8,128)S(1)}, u32[]{:S(2)}, u32[]{:S(2)}) %collective-permute-start.11) | collective-permute-done | bytes 65568 | tf_op jit(solution)/shard_map/ppermute | solution.py:385
  41.1 0.0 collective-permute-done.9.other_ref
  41.1 0.3 shard_map.60
  41.5 0.1 collective-permute-start.12
  41.5 0.6 %collective-permute-start.13 = (f32[2,64,128]{2,1,0:T(8,128)S(1)}, f32[2,64,128]{2,1,0:T(8,128)S(1)}, u32[]{:S(2)}, u32[]{:S(2)}) collective-permute-start(f32[2,64,128]{2,1,0:T(8,128)S(1)} %get-tuple-element.52), channel_id=1, source_target_pairs={{0,2},{4,6},{2,0},{6,4},{1,3},{5,7},{3,1},{7,5},{8,10},{12,14},{10... | collective-permute-start | bytes 196616 | tf_op jit(solution)/shard_map/ppermute | solution.py:392
  42.1 3.1 %collective-permute-done.12 = f32[2,64,128]{2,1,0:T(8,128)S(1)} collective-permute-done((f32[2,64,128]{2,1,0:T(8,128)S(1)}, f32[2,64,128]{2,1,0:T(8,128)S(1)}, u32[]{:S(2)}, u32[]{:S(2)}) %collective-permute-start.12) | collective-permute-done | bytes 65568 | tf_op jit(solution)/shard_map/ppermute | solution.py:392
  45.2 0.0 collective-permute-done.13
  45.2 0.7 %fusion = f32[1,2,128,128]{3,2,1,0:T(8,128)} fusion(f32[2,128,128]{2,1,0:T(8,128)S(1)} %get-tuple-element.50, f32[2,64,128]{2,1,0:T(8,128)S(1)} %get-tuple-element.54, f32[2,64,128]{2,1,0:T(8,128)S(1)} %get-tuple-element.53), kind=kLoop, calls=%fused_computation.1 | loop fusion | flops 65536 | bytes 393216 | tf_op jit(solution)/shard_map/broadcast_in_dim | solution.py:397
  (2 shorter events, 0.0 us)
Async XLA Ops:
  0.0 18.8 %copy-start = (bf16[8,256,256]{2,1,0:T(8,128)(2,1)S(1)}, bf16[8,256,256]{2,1,0:T(8,128)(2,1)}, u32[]{:S(2)}) copy-start(bf16[8,256,256]{2,1,0:T(8,128)(2,1)} %constant.21.clone.table_ref.refs_4_) | copy-start | bytes 3145732
  0.0 18.8 %copy-start.1 = (f32[4,2,128,128]{3,2,1,0:T(8,128)S(1)}, f32[4,2,128,128]{3,2,1,0:T(8,128)}, u32[]{:S(2)}) copy-start(f32[4,2,128,128]{3,2,1,0:T(8,128)} %refs_6_.1) | copy-start | bytes 1572868
  1.6 8.3 %collective-permute-start = (f32[4,2,64,128]{3,2,1,0:T(8,128)S(1)}, f32[4,2,64,128]{3,2,1,0:T(8,128)S(1)}, u32[]{:S(2)}, u32[]{:S(2)}) collective-permute-start(f32[4,2,64,128]{3,2,1,0:T(8,128)S(1)} %get-tuple-element.31), channel_id=1, source_target_pairs={{0,2},{4,6},{2,0},{6,4},{1,3},{5,7},{3,1},{7,5},{8,10},{12,14},{10... | collective-permute-start | bytes 786440 | tf_op jit(solution)/shard_map/ppermute | solution.py:346
  2.1 9.2 %collective-permute-start.1 = (f32[4,2,64,128]{3,2,1,0:T(8,128)S(1)}, f32[4,2,64,128]{3,2,1,0:T(8,128)S(1)}, u32[]{:S(2)}, u32[]{:S(2)}) collective-permute-start(f32[4,2,64,128]{3,2,1,0:T(8,128)S(1)} %get-tuple-element.32), channel_id=1, source_target_pairs={{2,4},{6,0},{4,2},{0,6},{3,5},{7,1},{5,3},{1,7},{10,12},{14,8},{12... | collective-permute-start | bytes 786440 | tf_op jit(solution)/shard_map/ppermute | solution.py:346
  4.7 8.3 %collective-permute-start.2 = (f32[4,128,128]{2,1,0:T(8,128)S(1)}, f32[4,128,128]{2,1,0:T(8,128)S(1)}, u32[]{:S(2)}, u32[]{:S(2)}) collective-permute-start(f32[4,128,128]{2,1,0:T(8,128)S(1)} %get-tuple-element.33), channel_id=1, source_target_pairs={{0,1},{1,0},{2,3},{3,2},{4,5},{5,4},{6,7},{7,6},{8,9},{9,8},{10,11... | collective-permute-start | bytes 786440 | tf_op jit(solution)/shard_map/ppermute | solution.py:345
  6.2 10.0 %collective-permute-start.5 = (f32[2,2,128,128]{3,2,1,0:T(8,128)S(1)}, f32[2,2,128,128]{3,2,1,0:T(8,128)S(1)}, u32[]{:S(2)}, u32[]{:S(2)}) collective-permute-start(f32[2,2,128,128]{3,2,1,0:T(8,128)S(1)} %get-tuple-element.37), channel_id=1, source_target_pairs={{0,24},{8,16},{16,8},{24,0},{1,25},{9,17},{17,9},{25,1},{2,26},{10... | collective-permute-start | bytes 786440 | tf_op jit(solution)/shard_map/ppermute | solution.py:344
  13.0 3.2 %collective-permute-start.3 = (f32[1,4,64,128]{3,2,1,0:T(8,128)S(1)}, f32[1,4,64,128]{3,2,1,0:T(8,128)S(1)}, u32[]{:S(2)}, u32[]{:S(2)}) collective-permute-start(f32[1,4,64,128]{3,2,1,0:T(8,128)S(1)} %get-tuple-element.34), channel_id=1, source_target_pairs={{0,2},{4,6},{2,0},{6,4},{1,3},{5,7},{3,1},{7,5},{8,10},{12,14},{10... | collective-permute-start | bytes 393224 | tf_op jit(solution)/shard_map/ppermute | solution.py:352
  13.1 5.3 %collective-permute-start.4 = (f32[1,4,64,128]{3,2,1,0:T(8,128)S(1)}, f32[1,4,64,128]{3,2,1,0:T(8,128)S(1)}, u32[]{:S(2)}, u32[]{:S(2)}) collective-permute-start(f32[1,4,64,128]{3,2,1,0:T(8,128)S(1)} %get-tuple-element.35), channel_id=1, source_target_pairs={{2,4},{6,0},{4,2},{0,6},{3,5},{7,1},{5,3},{1,7},{10,12},{14,8},{12... | collective-permute-start | bytes 393224 | tf_op jit(solution)/shard_map/ppermute | solution.py:352
  18.4 3.2 %collective-permute-start.6 = (f32[2,2,128,128]{3,2,1,0:T(8,128)S(1)}, f32[2,2,128,128]{3,2,1,0:T(8,128)S(1)}, u32[]{:S(2)}, u32[]{:S(2)}) collective-permute-start(f32[2,2,128,128]{3,2,1,0:T(8,128)S(1)} %collective-permute-done.5.refs_0_.refs_7_), channel_id=1, source_target_pairs={{0,2},{4,6},{2,0},{6,4},{1,3},{5,7},{3,1},{7,5},{8,10},{12,14},{10... | collective-permute-start | bytes 786440 | tf_op jit(solution)/shard_map/ppermute | solution.py:354
  21.6 8.6 %copy-start.2 = (f32[1,1,1,128,128]{4,3,2,1,0:T(8,128)S(1)}, f32[1,1,1,128,128]{4,3,2,1,0:T(8,128)}, u32[]{:S(2)}) copy-start(f32[1,1,1,128,128]{4,3,2,1,0:T(8,128)} %param.8) | copy-start | bytes 196612
  23.8 6.4 %collective-permute-start.8 = (f32[128,128]{1,0:T(8,128)S(1)}, f32[128,128]{1,0:T(8,128)S(1)}, u32[]{:S(2)}, u32[]{:S(2)}) collective-permute-start(f32[128,128]{1,0:T(8,128)S(1)} %get-tuple-element.40.refs_2_), channel_id=1, source_target_pairs={{0,8},{16,24},{8,0},{24,16},{1,9},{17,25},{9,1},{25,17},{2,10},{18... | collective-permute-start | bytes 196616 | tf_op jit(solution)/shard_map/ppermute | solution.py:369
  26.6 3.7 %collective-permute-start.7 = (s32[2,8,128]{2,1,0:T(8,128)S(1)}, s32[2,8,128]{2,1,0:T(8,128)S(1)}, u32[]{:S(2)}, u32[]{:S(2)}) collective-permute-start(s32[2,8,128]{2,1,0:T(8,128)S(1)} %get-tuple-element.41.refs_0_.place_ref), channel_id=1, source_target_pairs={{0,1},{1,0},{2,3},{3,2},{4,5},{5,4},{6,7},{7,6},{8,9},{9,8},{10,11... | collective-permute-start | bytes 24584 | tf_op jit(solution)/shard_map/ppermute | solution.py:371
  34.5 6.6 %collective-permute-start.9 = (f32[2,128,128]{2,1,0:T(8,128)S(1)}, f32[2,128,128]{2,1,0:T(8,128)S(1)}, u32[]{:S(2)}, u32[]{:S(2)}) collective-permute-start(f32[2,128,128]{2,1,0:T(8,128)S(1)} %get-tuple-element.47), channel_id=1, source_target_pairs={{0,8},{16,24},{8,0},{24,16},{1,9},{17,25},{9,1},{25,17},{2,10},{18... | collective-permute-start | bytes 393224 | tf_op jit(solution)/shard_map/ppermute | solution.py:380
  35.4 4.7 %collective-permute-start.10 = (f32[128,128]{1,0:T(8,128)S(1)}, f32[128,128]{1,0:T(8,128)S(1)}, u32[]{:S(2)}, u32[]{:S(2)}) collective-permute-start(f32[128,128]{1,0:T(8,128)S(1)} %get-tuple-element.48), channel_id=1, source_target_pairs={{0,1},{1,0},{2,3},{3,2},{4,5},{5,4},{6,7},{7,6},{8,9},{9,8},{10,11... | collective-permute-start | bytes 196616 | tf_op jit(solution)/shard_map/ppermute | solution.py:381
  35.9 5.2 %collective-permute-start.11 = (f32[128,128]{1,0:T(8,128)S(1)}, f32[128,128]{1,0:T(8,128)S(1)}, u32[]{:S(2)}, u32[]{:S(2)}) collective-permute-start(f32[128,128]{1,0:T(8,128)S(1)} %get-tuple-element.49), channel_id=1, source_target_pairs={{0,9},{1,8},{16,25},{17,24},{8,1},{9,0},{24,17},{25,16},{2,11},{3,... | collective-permute-start | bytes 196616 | tf_op jit(solution)/shard_map/ppermute | solution.py:385
  41.5 3.8 %collective-permute-start.12 = (f32[2,64,128]{2,1,0:T(8,128)S(1)}, f32[2,64,128]{2,1,0:T(8,128)S(1)}, u32[]{:S(2)}, u32[]{:S(2)}) collective-permute-start(f32[2,64,128]{2,1,0:T(8,128)S(1)} %get-tuple-element.51), channel_id=1, source_target_pairs={{2,4},{6,0},{4,2},{0,6},{3,5},{7,1},{5,3},{1,7},{10,12},{14,8},{12... | collective-permute-start | bytes 196616 | tf_op jit(solution)/shard_map/ppermute | solution.py:392
  41.5 3.7 %collective-permute-start.13 = (f32[2,64,128]{2,1,0:T(8,128)S(1)}, f32[2,64,128]{2,1,0:T(8,128)S(1)}, u32[]{:S(2)}, u32[]{:S(2)}) collective-permute-start(f32[2,64,128]{2,1,0:T(8,128)S(1)} %get-tuple-element.52), channel_id=1, source_target_pairs={{0,2},{4,6},{2,0},{6,4},{1,3},{5,7},{3,1},{7,5},{8,10},{12,14},{10... | collective-permute-start | bytes 196616 | tf_op jit(solution)/shard_map/ppermute | solution.py:392

commit v4 on v3

--- a/solution.py
+++ b/solution.py
@@ -102,16 +102,16 @@
     column = lax.axis_index(column_axis)
     whole = [pltpu.make_async_copy(tile_hbm.at[s], tile_ref.at[s], sems.at[s]) for s in range(slices)]
     sources = [(probe_hbm.at[pl.ds(lax.rem(row, SHARES) * share, share)], part_ref)]
-    for edge, edge_ref in enumerate(edge_refs):
-        first = half_rows(det, row_parity, edge)
-        sources.append((tile_hbm.at[:, :, pl.ds(first, det // 2)], edge_ref))
     sources.append((place_hbm, place_smem))
     others = [pltpu.make_async_copy(*ends, sems.at[slices + i]) for i, ends in enumerate(sources)]
-    for move in whole + others:
+    for move in others + whole:
         move.start()
     lower = iota((det, det), 1) < det // 2
+    firsts = [half_rows(det, row_parity, edge) for edge in range(2)]
     for s in range(slices):
         whole[s].wait()
+        for first, edge_ref in zip(firsts, edge_refs):
+            edge_ref[s] = tile_ref[s, :, pl.ds(first, det // 2)]
         for parity, message_ref in zip(parities, message_refs):
             right = is_right(column, parity)
             real, imag = tile_ref[s, 0], tile_ref[s, 1]
@@ -338,7 +338,7 @@
         ]
         + [shape(slices, det, det)] * count,
         [pltpu.with_memory_space_constraint(x, pltpu.HBM) for x in (positions.reshape(2), object_slices, probe_modes)],
-        scratch=[pltpu.SMEM((2,), jnp.int32), pltpu.SemaphoreType.DMA((slices + 4,))],
+        scratch=[pltpu.SMEM((2,), jnp.int32), pltpu.SemaphoreType.DMA((slices + 2,))],
         in_spec=HBM_SPEC,
     )
     fetched = lax.ppermute(part, "mode", mirror)

time: 46.1 us -> 46.1 us (level)
  no operation moved by 1% of the time
where the time goes in v4:
time: 46.1 us; the launch traced here: 46 us
  waiting for transfers between devices  17.2 us (37%)
  starting transfers between devices  16.7 us (36%)
  Pallas kernels  11.3 us (25%)
  other arithmetic  0.69 us (1%)
    pallas_call x6, Pallas kernels, call(): pl.pallas_call(kernel, out_shape=outs, in_specs=[in_spec] * len(operands)...  11.3 us
    ppermute x6, waiting for transfers between devices, body(): lax.ppermute(block, 'ty', edges(height, edge))  6.77 us
    ppermute x6, starting transfers between devices, body(): lax.ppermute(block, 'ty', edges(height, edge))  4.35 us
    ppermute x2, waiting for transfers between devices, body(): lax.ppermute(block, 'tx', edges(width, parity))  3.77 us
    ppermute x1, starting transfers between devices, body(): fetched = lax.ppermute(part, 'mode', mirror)  3.6 us
    ppermute x1, waiting for transfers between devices, body(): lax.ppermute(place, 'tx', edges(width, parity))  3.05 us
    ppermute x1, starting transfers between devices, body(): other = lax.ppermute(mine, 'mode', neighbour)  2.72 us
    ppermute x1, waiting for transfers between devices, body(): fetched = lax.ppermute(part, 'mode', mirror)  2.64 us
  transfers between devices with their start and end apart: 14, of which 8 were waited for; matrix products, arithmetic and copies ran while one was open for 0% of the time, Pallas kernels for 6%

profile of v4, /device:TPU:0, one launch (start us, length us, event | category | flops | bytes accessed | tf_op | source)
XLA Modules:
  0.0 46.0 jit_solution(11944402495940538557)
XLA Ops:
  0.0 0.0 copy-start
  0.0 0.0 copy-start.1
  0.0 1.6 %shard_map.55 = (s32[2,8,128]{2,1,0:T(8,128)S(1)}, f32[4,2,128,128]{3,2,1,0:T(8,128)S(1)}, f32[2,2,128,128]{3,2,1,0:T(8,128)S(1)}, f32[4,2,64,128]{3,2,1,0:T(8,1...) custom-call(s32[2]{0:T(128)} %bitcast.5, f32[4,2,128,128]{3,2,1,0:T(8,128)} %tile_hbm.1, ...), custom_call_target="tpu_custom_call" | custom-call | tf_op jit(solution)/shard_map/pallas_call | solution.py:303
  1.6 0.5 %collective-permute-start = (f32[4,2,64,128]{3,2,1,0:T(8,128)S(1)}, f32[4,2,64,128]{3,2,1,0:T(8,128)S(1)}, u32[]{:S(2)}, u32[]{:S(2)}) collective-permute-start(f32[4,2,64,128]{3,2,1,0:T(8,128)S(1)} %get-tuple-element.31), channel_id=1, source_target_pairs={{0,2},{4,6},{2,0},{6,4},{1,3},{5,7},{3,1},{7,5},{8,10},{12,14},{10... | collective-permute-start | bytes 786440 | tf_op jit(solution)/shard_map/ppermute | solution.py:346
  2.1 2.6 %collective-permute-start.1 = (f32[4,2,64,128]{3,2,1,0:T(8,128)S(1)}, f32[4,2,64,128]{3,2,1,0:T(8,128)S(1)}, u32[]{:S(2)}, u32[]{:S(2)}) collective-permute-start(f32[4,2,64,128]{3,2,1,0:T(8,128)S(1)} %get-tuple-element.32), channel_id=1, source_target_pairs={{2,4},{6,0},{4,2},{0,6},{3,5},{7,1},{5,3},{1,7},{10,12},{14,8},{12... | collective-permute-start | bytes 786440 | tf_op jit(solution)/shard_map/ppermute | solution.py:346
  4.8 1.5 %collective-permute-start.2 = (f32[4,128,128]{2,1,0:T(8,128)S(1)}, f32[4,128,128]{2,1,0:T(8,128)S(1)}, u32[]{:S(2)}, u32[]{:S(2)}) collective-permute-start(f32[4,128,128]{2,1,0:T(8,128)S(1)} %get-tuple-element.33), channel_id=1, source_target_pairs={{0,1},{1,0},{2,3},{3,2},{4,5},{5,4},{6,7},{7,6},{8,9},{9,8},{10,11... | collective-permute-start | bytes 786440 | tf_op jit(solution)/shard_map/ppermute | solution.py:345
  6.3 3.6 %collective-permute-start.5 = (f32[2,2,128,128]{3,2,1,0:T(8,128)S(1)}, f32[2,2,128,128]{3,2,1,0:T(8,128)S(1)}, u32[]{:S(2)}, u32[]{:S(2)}) collective-permute-start(f32[2,2,128,128]{3,2,1,0:T(8,128)S(1)} %get-tuple-element.37), channel_id=1, source_target_pairs={{0,24},{8,16},{16,8},{24,0},{1,25},{9,17},{17,9},{25,1},{2,26},{10... | collective-permute-start | bytes 786440 | tf_op jit(solution)/shard_map/ppermute | solution.py:344
  9.9 0.0 collective-permute-done.refs_1_.refs_2_
  9.9 1.5 %collective-permute-done.1.refs_2_.refs_3_ = f32[4,2,64,128]{3,2,1,0:T(8,128)S(1)} collective-permute-done((f32[4,2,64,128]{3,2,1,0:T(8,128)S(1)}, f32[4,2,64,128]{3,2,1,0:T(8,128)S(1)}, u32[]{:S(2)}, u32[]{:S(2)}) %collective-permute-start.1) | collective-permute-done | bytes 262176 | tf_op jit(solution)/shard_map/ppermute | solution.py:346
  11.4 1.7 %collective-permute-done.2.refs_0_.refs_6_ = f32[4,128,128]{2,1,0:T(8,128)S(1)} collective-permute-done((f32[4,128,128]{2,1,0:T(8,128)S(1)}, f32[4,128,128]{2,1,0:T(8,128)S(1)}, u32[]{:S(2)}, u32[]{:S(2)}) %collective-permute-start.2) | collective-permute-done | bytes 262176 | tf_op jit(solution)/shard_map/ppermute | solution.py:345
  13.1 0.1 collective-permute-start.3
  13.2 0.4 collective-permute-start.4
  13.6 2.6 %collective-permute-done.5.refs_0_.refs_7_ = f32[2,2,128,128]{3,2,1,0:T(8,128)S(1)} collective-permute-done((f32[2,2,128,128]{3,2,1,0:T(8,128)S(1)}, f32[2,2,128,128]{3,2,1,0:T(8,128)S(1)}, u32[]{:S(2)}, u32[]{:S(2)}) %collective-permute-start.5) | collective-permute-done | bytes 262176 | tf_op jit(solution)/shard_map/ppermute | solution.py:344
  16.2 0.0 collective-permute-done.3.refs_4_
  16.2 2.2 %collective-permute-done.4.refs_5_ = f32[1,4,64,128]{3,2,1,0:T(8,128)S(1)} collective-permute-done((f32[1,4,64,128]{3,2,1,0:T(8,128)S(1)}, f32[1,4,64,128]{3,2,1,0:T(8,128)S(1)}, u32[]{:S(2)}, u32[]{:S(2)}) %collective-permute-start.4) | collective-permute-done | bytes 131104 | tf_op jit(solution)/shard_map/ppermute | solution.py:352
  18.5 0.4 collective-permute-start.6
  18.8 0.0 copy-done
  18.8 0.0 copy-done.1
  18.9 2.8 %shard_map.57 = (f32[4,2,128,128]{3,2,1,0:T(8,128)S(1)}, f32[3,4,2,128,128]{4,3,2,1,0:T(8,128)S(1)}, f32[4,2,128,128]{3,2,1,0:T(8,128)S(1)}, f32[128,128]{1,0:T(8,128)S(1)}) custom-call(bf16[8,256,256]{2,1,0:T(8,128)(2,1)S(1)} %copy-done, f32[4,2,128,128]{3,2,1,0:T(8,128)S(1)} %copy-done.1, s32[2,8,128]{2,1,0:T(8,128)S(1)} %get-tuple-element.41.refs_0_.place_ref, ...), custom_call_target="tpu_custom_call" | custom-call | tf_op jit(solution)/shard_map/pallas_call | solution.py:303
  21.7 0.0 copy-start.2
  21.7 0.0 collective-permute-done.6.refs_1_.refs_8_
  21.7 2.2 %shard_map.58 = (f32[3,4,2,128,128]{4,3,2,1,0:T(8,128)S(1)}, f32[4,2,128,128]{3,2,1,0:T(8,128)S(1)}, f32[128,128]{1,0:T(8,128)S(1)}) custom-call(f32[4,2,128,128]{3,2,1,0:T(8,128)S(1)} %get-tuple-element.36.window_ref.refs_5_, bf16[8,256,256]{2,1,0:T(8,128)(2,1)S(1)} %copy-done, f32[2,2,128,128]{3,2,1,0:T(8,128)S(1)} %collective-permute-done.5.refs_0_.refs_7_, ...), custom_call_target="tpu_custom_call" | custom-call | tf_op jit(solution)/shard_map/pallas_call | solution.py:303
  23.9 2.7 %collective-permute-start.8 = (f32[128,128]{1,0:T(8,128)S(1)}, f32[128,128]{1,0:T(8,128)S(1)}, u32[]{:S(2)}, u32[]{:S(2)}) collective-permute-start(f32[128,128]{1,0:T(8,128)S(1)} %get-tuple-element.40.refs_2_), channel_id=1, source_target_pairs={{0,8},{16,24},{8,0},{24,16},{1,9},{17,25},{9,1},{25,17},{2,10},{18... | collective-permute-start | bytes 196616 | tf_op jit(solution)/shard_map/ppermute | solution.py:369
  26.6 0.6 %collective-permute-start.7 = (s32[2,8,128]{2,1,0:T(8,128)S(1)}, s32[2,8,128]{2,1,0:T(8,128)S(1)}, u32[]{:S(2)}, u32[]{:S(2)}) collective-permute-start(s32[2,8,128]{2,1,0:T(8,128)S(1)} %get-tuple-element.41.refs_0_.place_ref), channel_id=1, source_target_pairs={{0,1},{1,0},{2,3},{3,2},{4,5},{5,4},{6,7},{7,6},{8,9},{9,8},{10,11... | collective-permute-start | bytes 24584 | tf_op jit(solution)/shard_map/ppermute | solution.py:371
  27.2 3.0 %collective-permute-done.7.refs_0_ = s32[2,8,128]{2,1,0:T(8,128)S(1)} collective-permute-done((s32[2,8,128]{2,1,0:T(8,128)S(1)}, s32[2,8,128]{2,1,0:T(8,128)S(1)}, u32[]{:S(2)}, u32[]{:S(2)}) %collective-permute-start.7) | collective-permute-done | bytes 8224 | tf_op jit(solution)/shard_map/ppermute | solution.py:371
  30.3 0.0 collective-permute-done.8.refs_3_
  30.3 0.0 copy-done.2
  30.3 4.3 %shard_map.59 = (f32[2,128,128]{2,1,0:T(8,128)S(1)}, f32[2,128,128]{2,1,0:T(8,128)S(1)}, f32[128,128]{1,0:T(8,128)S(1)}, f32[128,128]{1,0:T(8,128)S(1)}) custom-call(s32[2,8,128]{2,1,0:T(8,128)S(1)} %get-tuple-element.41.refs_0_.place_ref, s32[2,8,128]{2,1,0:T(8,128)S(1)} %collective-permute-done.7.refs_0_, f32[128,128]{1,0:T(8,128)S(1)} %bitcast.4, ...), custom_call_target="tpu_custom_call" | custom-call | tf_op jit(solution)/shard_map/pallas_call | solution.py:303
  34.5 0.9 %collective-permute-start.9 = (f32[2,128,128]{2,1,0:T(8,128)S(1)}, f32[2,128,128]{2,1,0:T(8,128)S(1)}, u32[]{:S(2)}, u32[]{:S(2)}) collective-permute-start(f32[2,128,128]{2,1,0:T(8,128)S(1)} %get-tuple-element.47), channel_id=1, source_target_pairs={{0,8},{16,24},{8,0},{24,16},{1,9},{17,25},{9,1},{25,17},{2,10},{18... | collective-permute-start | bytes 393224 | tf_op jit(solution)/shard_map/ppermute | solution.py:380
  35.4 0.6 %collective-permute-start.10 = (f32[128,128]{1,0:T(8,128)S(1)}, f32[128,128]{1,0:T(8,128)S(1)}, u32[]{:S(2)}, u32[]{:S(2)}) collective-permute-start(f32[128,128]{1,0:T(8,128)S(1)} %get-tuple-element.48), channel_id=1, source_target_pairs={{0,1},{1,0},{2,3},{3,2},{4,5},{5,4},{6,7},{7,6},{8,9},{9,8},{10,11... | collective-permute-start | bytes 196616 | tf_op jit(solution)/shard_map/ppermute | solution.py:381
  36.0 2.1 %collective-permute-start.11 = (f32[128,128]{1,0:T(8,128)S(1)}, f32[128,128]{1,0:T(8,128)S(1)}, u32[]{:S(2)}, u32[]{:S(2)}) collective-permute-start(f32[128,128]{1,0:T(8,128)S(1)} %get-tuple-element.49), channel_id=1, source_target_pairs={{0,9},{1,8},{16,25},{17,24},{8,1},{9,0},{24,17},{25,16},{2,11},{3,... | collective-permute-start | bytes 196616 | tf_op jit(solution)/shard_map/ppermute | solution.py:385
  38.1 2.1 %collective-permute-done.10.refs_1_ = f32[128,128]{1,0:T(8,128)S(1)} collective-permute-done((f32[128,128]{1,0:T(8,128)S(1)}, f32[128,128]{1,0:T(8,128)S(1)}, u32[]{:S(2)}, u32[]{:S(2)}) %collective-permute-start.10) | collective-permute-done | bytes 65568 | tf_op jit(solution)/shard_map/ppermute | solution.py:381
  40.2 1.0 %collective-permute-done.11.refs_2_ = f32[128,128]{1,0:T(8,128)S(1)} collective-permute-done((f32[128,128]{1,0:T(8,128)S(1)}, f32[128,128]{1,0:T(8,128)S(1)}, u32[]{:S(2)}, u32[]{:S(2)}) %collective-permute-start.11) | collective-permute-done | bytes 65568 | tf_op jit(solution)/shard_map/ppermute | solution.py:385
  41.2 0.0 collective-permute-done.9.other_ref
  41.2 0.3 shard_map.60
  41.5 0.1 collective-permute-start.12
  41.6 0.6 %collective-permute-start.13 = (f32[2,64,128]{2,1,0:T(8,128)S(1)}, f32[2,64,128]{2,1,0:T(8,128)S(1)}, u32[]{:S(2)}, u32[]{:S(2)}) collective-permute-start(f32[2,64,128]{2,1,0:T(8,128)S(1)} %get-tuple-element.52), channel_id=1, source_target_pairs={{0,2},{4,6},{2,0},{6,4},{1,3},{5,7},{3,1},{7,5},{8,10},{12,14},{10... | collective-permute-start | bytes 196616 | tf_op jit(solution)/shard_map/ppermute | solution.py:392
  42.2 3.1 %collective-permute-done.12 = f32[2,64,128]{2,1,0:T(8,128)S(1)} collective-permute-done((f32[2,64,128]{2,1,0:T(8,128)S(1)}, f32[2,64,128]{2,1,0:T(8,128)S(1)}, u32[]{:S(2)}, u32[]{:S(2)}) %collective-permute-start.12) | collective-permute-done | bytes 65568 | tf_op jit(solution)/shard_map/ppermute | solution.py:392
  45.3 0.0 collective-permute-done.13
  45.3 0.7 %fusion = f32[1,2,128,128]{3,2,1,0:T(8,128)} fusion(f32[2,128,128]{2,1,0:T(8,128)S(1)} %get-tuple-element.50, f32[2,64,128]{2,1,0:T(8,128)S(1)} %get-tuple-element.54, f32[2,64,128]{2,1,0:T(8,128)S(1)} %get-tuple-element.53), kind=kLoop, calls=%fused_computation.1 | loop fusion | flops 65536 | bytes 393216 | tf_op jit(solution)/shard_map/broadcast_in_dim | solution.py:397
  (2 shorter events, 0.0 us)
Async XLA Ops:
  0.0 18.8 %copy-start = (bf16[8,256,256]{2,1,0:T(8,128)(2,1)S(1)}, bf16[8,256,256]{2,1,0:T(8,128)(2,1)}, u32[]{:S(2)}) copy-start(bf16[8,256,256]{2,1,0:T(8,128)(2,1)} %constant.21.clone.table_ref.refs_4_) | copy-start | bytes 3145732
  0.0 18.8 %copy-start.1 = (f32[4,2,128,128]{3,2,1,0:T(8,128)S(1)}, f32[4,2,128,128]{3,2,1,0:T(8,128)}, u32[]{:S(2)}) copy-start(f32[4,2,128,128]{3,2,1,0:T(8,128)} %refs_6_.1) | copy-start | bytes 1572868
  1.6 8.3 %collective-permute-start = (f32[4,2,64,128]{3,2,1,0:T(8,128)S(1)}, f32[4,2,64,128]{3,2,1,0:T(8,128)S(1)}, u32[]{:S(2)}, u32[]{:S(2)}) collective-permute-start(f32[4,2,64,128]{3,2,1,0:T(8,128)S(1)} %get-tuple-element.31), channel_id=1, source_target_pairs={{0,2},{4,6},{2,0},{6,4},{1,3},{5,7},{3,1},{7,5},{8,10},{12,14},{10... | collective-permute-start | bytes 786440 | tf_op jit(solution)/shard_map/ppermute | solution.py:346
  2.1 9.2 %collective-permute-start.1 = (f32[4,2,64,128]{3,2,1,0:T(8,128)S(1)}, f32[4,2,64,128]{3,2,1,0:T(8,128)S(1)}, u32[]{:S(2)}, u32[]{:S(2)}) collective-permute-start(f32[4,2,64,128]{3,2,1,0:T(8,128)S(1)} %get-tuple-element.32), channel_id=1, source_target_pairs={{2,4},{6,0},{4,2},{0,6},{3,5},{7,1},{5,3},{1,7},{10,12},{14,8},{12... | collective-permute-start | bytes 786440 | tf_op jit(solution)/shard_map/ppermute | solution.py:346
  4.8 8.3 %collective-permute-start.2 = (f32[4,128,128]{2,1,0:T(8,128)S(1)}, f32[4,128,128]{2,1,0:T(8,128)S(1)}, u32[]{:S(2)}, u32[]{:S(2)}) collective-permute-start(f32[4,128,128]{2,1,0:T(8,128)S(1)} %get-tuple-element.33), channel_id=1, source_target_pairs={{0,1},{1,0},{2,3},{3,2},{4,5},{5,4},{6,7},{7,6},{8,9},{9,8},{10,11... | collective-permute-start | bytes 786440 | tf_op jit(solution)/shard_map/ppermute | solution.py:345
  6.3 10.0 %collective-permute-start.5 = (f32[2,2,128,128]{3,2,1,0:T(8,128)S(1)}, f32[2,2,128,128]{3,2,1,0:T(8,128)S(1)}, u32[]{:S(2)}, u32[]{:S(2)}) collective-permute-start(f32[2,2,128,128]{3,2,1,0:T(8,128)S(1)} %get-tuple-element.37), channel_id=1, source_target_pairs={{0,24},{8,16},{16,8},{24,0},{1,25},{9,17},{17,9},{25,1},{2,26},{10... | collective-permute-start | bytes 786440 | tf_op jit(solution)/shard_map/ppermute | solution.py:344
  13.1 3.2 %collective-permute-start.3 = (f32[1,4,64,128]{3,2,1,0:T(8,128)S(1)}, f32[1,4,64,128]{3,2,1,0:T(8,128)S(1)}, u32[]{:S(2)}, u32[]{:S(2)}) collective-permute-start(f32[1,4,64,128]{3,2,1,0:T(8,128)S(1)} %get-tuple-element.34), channel_id=1, source_target_pairs={{0,2},{4,6},{2,0},{6,4},{1,3},{5,7},{3,1},{7,5},{8,10},{12,14},{10... | collective-permute-start | bytes 393224 | tf_op jit(solution)/shard_map/ppermute | solution.py:352
  13.2 5.3 %collective-permute-start.4 = (f32[1,4,64,128]{3,2,1,0:T(8,128)S(1)}, f32[1,4,64,128]{3,2,1,0:T(8,128)S(1)}, u32[]{:S(2)}, u32[]{:S(2)}) collective-permute-start(f32[1,4,64,128]{3,2,1,0:T(8,128)S(1)} %get-tuple-element.35), channel_id=1, source_target_pairs={{2,4},{6,0},{4,2},{0,6},{3,5},{7,1},{5,3},{1,7},{10,12},{14,8},{12... | collective-permute-start | bytes 393224 | tf_op jit(solution)/shard_map/ppermute | solution.py:352
  18.5 3.2 %collective-permute-start.6 = (f32[2,2,128,128]{3,2,1,0:T(8,128)S(1)}, f32[2,2,128,128]{3,2,1,0:T(8,128)S(1)}, u32[]{:S(2)}, u32[]{:S(2)}) collective-permute-start(f32[2,2,128,128]{3,2,1,0:T(8,128)S(1)} %collective-permute-done.5.refs_0_.refs_7_), channel_id=1, source_target_pairs={{0,2},{4,6},{2,0},{6,4},{1,3},{5,7},{3,1},{7,5},{8,10},{12,14},{10... | collective-permute-start | bytes 786440 | tf_op jit(solution)/shard_map/ppermute | solution.py:354
  21.7 8.6 %copy-start.2 = (f32[1,1,1,128,128]{4,3,2,1,0:T(8,128)S(1)}, f32[1,1,1,128,128]{4,3,2,1,0:T(8,128)}, u32[]{:S(2)}) copy-start(f32[1,1,1,128,128]{4,3,2,1,0:T(8,128)} %param.8) | copy-start | bytes 196612
  23.9 6.4 %collective-permute-start.8 = (f32[128,128]{1,0:T(8,128)S(1)}, f32[128,128]{1,0:T(8,128)S(1)}, u32[]{:S(2)}, u32[]{:S(2)}) collective-permute-start(f32[128,128]{1,0:T(8,128)S(1)} %get-tuple-element.40.refs_2_), channel_id=1, source_target_pairs={{0,8},{16,24},{8,0},{24,16},{1,9},{17,25},{9,1},{25,17},{2,10},{18... | collective-permute-start | bytes 196616 | tf_op jit(solution)/shard_map/ppermute | solution.py:369
  26.6 3.7 %collective-permute-start.7 = (s32[2,8,128]{2,1,0:T(8,128)S(1)}, s32[2,8,128]{2,1,0:T(8,128)S(1)}, u32[]{:S(2)}, u32[]{:S(2)}) collective-permute-start(s32[2,8,128]{2,1,0:T(8,128)S(1)} %get-tuple-element.41.refs_0_.place_ref), channel_id=1, source_target_pairs={{0,1},{1,0},{2,3},{3,2},{4,5},{5,4},{6,7},{7,6},{8,9},{9,8},{10,11... | collective-permute-start | bytes 24584 | tf_op jit(solution)/shard_map/ppermute | solution.py:371
  34.5 6.6 %collective-permute-start.9 = (f32[2,128,128]{2,1,0:T(8,128)S(1)}, f32[2,128,128]{2,1,0:T(8,128)S(1)}, u32[]{:S(2)}, u32[]{:S(2)}) collective-permute-start(f32[2,128,128]{2,1,0:T(8,128)S(1)} %get-tuple-element.47), channel_id=1, source_target_pairs={{0,8},{16,24},{8,0},{24,16},{1,9},{17,25},{9,1},{25,17},{2,10},{18... | collective-permute-start | bytes 393224 | tf_op jit(solution)/shard_map/ppermute | solution.py:380
  35.4 4.7 %collective-permute-start.10 = (f32[128,128]{1,0:T(8,128)S(1)}, f32[128,128]{1,0:T(8,128)S(1)}, u32[]{:S(2)}, u32[]{:S(2)}) collective-permute-start(f32[128,128]{1,0:T(8,128)S(1)} %get-tuple-element.48), channel_id=1, source_target_pairs={{0,1},{1,0},{2,3},{3,2},{4,5},{5,4},{6,7},{7,6},{8,9},{9,8},{10,11... | collective-permute-start | bytes 196616 | tf_op jit(solution)/shard_map/ppermute | solution.py:381
  36.0 5.2 %collective-permute-start.11 = (f32[128,128]{1,0:T(8,128)S(1)}, f32[128,128]{1,0:T(8,128)S(1)}, u32[]{:S(2)}, u32[]{:S(2)}) collective-permute-start(f32[128,128]{1,0:T(8,128)S(1)} %get-tuple-element.49), channel_id=1, source_target_pairs={{0,9},{1,8},{16,25},{17,24},{8,1},{9,0},{24,17},{25,16},{2,11},{3,... | collective-permute-start | bytes 196616 | tf_op jit(solution)/shard_map/ppermute | solution.py:385
  41.5 3.8 %collective-permute-start.12 = (f32[2,64,128]{2,1,0:T(8,128)S(1)}, f32[2,64,128]{2,1,0:T(8,128)S(1)}, u32[]{:S(2)}, u32[]{:S(2)}) collective-permute-start(f32[2,64,128]{2,1,0:T(8,128)S(1)} %get-tuple-element.51), channel_id=1, source_target_pairs={{2,4},{6,0},{4,2},{0,6},{3,5},{7,1},{5,3},{1,7},{10,12},{14,8},{12... | collective-permute-start | bytes 196616 | tf_op jit(solution)/shard_map/ppermute | solution.py:392
  41.6 3.7 %collective-permute-start.13 = (f32[2,64,128]{2,1,0:T(8,128)S(1)}, f32[2,64,128]{2,1,0:T(8,128)S(1)}, u32[]{:S(2)}, u32[]{:S(2)}) collective-permute-start(f32[2,64,128]{2,1,0:T(8,128)S(1)} %get-tuple-element.52), channel_id=1, source_target_pairs={{0,2},{4,6},{2,0},{6,4},{1,3},{5,7},{3,1},{7,5},{8,10},{12,14},{10... | collective-permute-start | bytes 196616 | tf_op jit(solution)/shard_map/ppermute | solution.py:392
